TPU v7x, 512 devices: a whole 4x8x8 slice. The times are simulated.
512 devices in a mesh: mem: 16 (over y, core), reg: 32 (over z, x).
Axes of the slice: x: 4, y: 8, z: 8, core: 2. Of those that a mesh axis runs over, the one named last changes fastest.
Arguments:
- background: bfloat16 [256, 16, 65536], P('mem', None, 'reg'), may hold values from -6 to 6
- observations: float32 [32, 32, 384], P('reg', 'mem'), may hold values from -6 to 6
- obs_coef: float32 [32, 32, 384], P('reg', 'mem'), may hold values from 0.5 to 1.5
- obs_rinv: float32 [32, 32, 384], P('reg', 'mem'), may hold values from 0.1 to 2
- obs_site: int32 [32, 32, 384], P('reg', 'mem'), may hold values from 0 to 1023
- obs_count: int32 [32, 32], P('reg', 'mem'), may hold values from 1 to 384, as said below
- neighbours: int32 [32, 32, 5], P('reg', 'mem'), may hold values from 0 to 8, as said below
Outputs:
- analysis: bfloat16 [256, 16, 65536], P('mem', None, 'reg')
Inputs may be any that keep to these rules, and one draw needn't show every extreme that they name: `obs_count`: block counts are uneven across regions; some block has all 384 slots live in every draw. `neighbours`: each row holds distinct codes, never 4; codes 0 and 8 appear in every draw.
All inputs are finite; a program needn't handle non-finite values. Where the computation divides by a largest or mean magnitude, that divisor is 1e-20 or more.
Results may differ from a plain program's by a relative error of at most 0.009.
Values may be sent and summed in bfloat16 or wider, within the bound.
A program may use at most 64 MiB of HBM per device.

v0:
```python
import jax
import jax.numpy as jnp
from jax import lax
from jax.sharding import PartitionSpec as P

NS_ITERS = 4


def with_halo(block, sides, width):
    for axis, dim in sides:
        count = lax.axis_size(axis)
        forward = [(i, i + 1) for i in range(count - 1)]
        forward.append((count - 1, 0))
        backward = [(target, source) for source, target in forward]
        low = lax.ppermute(
            lax.slice_in_dim(block, block.shape[dim] - width, None, axis=dim), axis, forward
        )
        high = lax.ppermute(lax.slice_in_dim(block, 0, width, axis=dim), axis, backward)
        block = jnp.concatenate([low, block, high], axis=dim)
    return block


def local_obs(block, obs_site, obs_coef, obs_rinv, obs_count, observed):
    widened = block.astype(jnp.float32)
    mean_state = jnp.mean(widened, axis=0)
    spread = (widened - mean_state).astype(jnp.bfloat16)
    predicted = obs_coef * jnp.take(widened, obs_site, axis=1)
    mean_pred = jnp.mean(predicted, axis=0)
    keep = (jnp.arange(obs_site.shape[0], dtype=jnp.int32) < obs_count).astype(jnp.float32)
    weight_root = jnp.sqrt(obs_rinv) * keep
    scaled = (weight_root * (predicted - mean_pred)).astype(jnp.bfloat16)
    misfit = weight_root * (observed - mean_pred)
    return (mean_state, spread, scaled, misfit)


def newton_root(matrix):
    identity = jnp.eye(matrix.shape[-1], dtype=jnp.float32)
    current = matrix
    inverse = jnp.broadcast_to(identity, matrix.shape)
    for _ in range(NS_ITERS):
        middle = 1.5 * identity - 0.5 * jnp.matmul(
            inverse, current, precision=lax.Precision.HIGHEST
        )
        current = jnp.matmul(current, middle, precision=lax.Precision.HIGHEST)
        inverse = jnp.matmul(middle, inverse, precision=lax.Precision.HIGHEST)
    return inverse


def transform(system, drive, ensemble):
    row_scale = jnp.max(jnp.sum(jnp.abs(system), axis=-1), axis=-1)
    half = newton_root(system / row_scale[..., None, None]) / jnp.sqrt(row_scale)[..., None, None]
    inner_part = jnp.matmul(half, drive[..., None], precision=lax.Precision.HIGHEST)
    mean_weight = jnp.matmul(half, inner_part, precision=lax.Precision.HIGHEST)[..., 0]
    weights = jnp.sqrt(jnp.float32(ensemble - 1)) * half + mean_weight[..., :, None]
    return weights.astype(jnp.bfloat16)


def per_device(background, observations, obs_coef, obs_rinv, obs_site, obs_count, neighbours):
    members = lax.all_to_all(background, "mem", split_axis=2, concat_axis=0, tiled=True)
    ensemble, variables, width = members.shape
    blocks_dev = obs_site.shape[1]
    block_cols = width // blocks_dev
    blocks = (
        members.reshape(ensemble, variables, blocks_dev, block_cols)
        .transpose(2, 0, 1, 3)
        .reshape(blocks_dev, ensemble, variables * block_cols)
    )
    mean_state, spread, scaled, misfit = jax.vmap(local_obs)(
        blocks, obs_site[0], obs_coef[0], obs_rinv[0], obs_count[0], observations[0]
    )
    codes = jnp.concatenate([jnp.full((blocks_dev, 1), 4, jnp.int32), neighbours[0]], axis=1)
    step_r = codes // 3
    step_s = codes % 3
    placed = step_r * (blocks_dev + 2) + jnp.arange(blocks_dev, dtype=jnp.int32)[:, None] + step_s
    taper = jnp.exp2(-(jnp.abs(step_r - 1) + jnp.abs(step_s - 1)).astype(jnp.float32))
    stacked = 3 * (blocks_dev + 2)
    rim_scaled, rim_misfit = (
        with_halo(scaled[None], (("mem", 1), ("reg", 0)), 1),
        with_halo(misfit[None].astype(jnp.bfloat16), (("mem", 1), ("reg", 0)), 1).astype(
            jnp.float32
        ),
    )
    near_scaled = rim_scaled.reshape(stacked, ensemble, rim_scaled.shape[-1])[placed]
    near_misfit = rim_misfit.reshape(stacked, rim_misfit.shape[-1])[placed]
    near_gram = jnp.einsum(
        "bnko,bnlo->bnkl", near_scaled, near_scaled, preferred_element_type=jnp.float32
    )
    near_drive = jnp.einsum(
        "bnko,bno->bnk",
        near_scaled,
        near_misfit,
        preferred_element_type=jnp.float32,
        precision=lax.Precision.HIGHEST,
    )
    identity = jnp.eye(ensemble, dtype=jnp.float32)
    system = (ensemble - 1.0) * identity + jnp.sum(taper[..., None, None] * near_gram, axis=1)
    drive = jnp.sum(taper[..., None] * near_drive, axis=1)
    weights = transform(system, drive, ensemble)
    update = jnp.einsum("bkj,bkf->bjf", weights, spread, preferred_element_type=jnp.float32)
    analysis = (mean_state[:, None, :] + update).astype(jnp.bfloat16)
    regrouped = (
        analysis.reshape(blocks_dev, ensemble, variables, block_cols)
        .transpose(1, 2, 0, 3)
        .reshape(ensemble, variables, width)
    )
    return lax.all_to_all(regrouped, "mem", split_axis=0, concat_axis=2, tiled=True)


def solution(mesh):
    in_specs = (
        P("mem", None, "reg"),
        P("reg", "mem", None),
        P("reg", "mem", None),
        P("reg", "mem", None),
        P("reg", "mem", None),
        P("reg", "mem"),
        P("reg", "mem", None),
    )
    out_specs = P("mem", None, "reg")
    return jax.shard_map(
        per_device, mesh=mesh, in_specs=in_specs, out_specs=out_specs, check_vma=False
    )
```

profile of v0, /device:TPU:1, one launch (start us, length us, event | category | flops | bytes accessed | tf_op | source)
XLA Modules:
  0.0 200.9 jit_solution(10561280689435217511)
XLA Ops:
  0.0 9.6 %copy.75 = bf16[16,16,2048]{1,0,2:T(8,128)(2,1)} copy(bf16[16,16,2048]{2,1,0:T(8,128)(2,1)} %param.7) | data formatting | bytes 2097152 | tf_op args[0]
  9.6 11.3 %reshape.229 = bf16[16,2,16384]{2,1,0:T(2,128)(2,1)} reshape(bf16[2048,16,16]{2,1,0:T(8,128)(2,1)} %bitcast.84) | data formatting | bytes 2097152
  20.9 10.5 %all-to-all-start = ((bf16[16,2,16384]{2,1,0:T(2,128)(2,1)}), bf16[16,2,16384]{2,1,0:T(2,128)(2,1)S(1)}, u32[]{:S(2)}, u32[]{:S(2)}) async-start(bf16[16,2,16384]{2,1,0:T(2,128)(2,1)} %reshape.229), calls=%async_computation | async-start | bytes 2097152 | tf_op jit(solution)/shard_map/all_to_all | solution.py:59
  31.8 0.6 pad_clamp_fusion
  32.3 0.7 fusion.11
  33.1 0.8 fusion.10
  33.9 0.6 compare_select_fusion.3
  34.5 24.8 %all-to-all-done = bf16[16,2,16384]{2,1,0:T(2,128)(2,1)S(1)} async-done(((bf16[16,2,16384]{2,1,0:T(2,128)(2,1)}), bf16[16,2,16384]{2,1,0:T(2,128)(2,1)S(1)}, u32[]{:S(2)}, u32[]{:S(2)}) %all-to-all-start) | async-done | bytes 1048608 | tf_op jit(solution)/shard_map/all_to_all | solution.py:59
  59.3 7.6 %reshape.230 = bf16[2048,16,16]{2,1,0:T(8,128)(2,1)} reshape(bf16[16,2,16384]{2,1,0:T(2,128)(2,1)S(1)} %all-to-all-done) | data formatting | bytes 2097152
  66.9 9.1 %copy.78 = f32[16,16,16,128]{3,1,0,2:T(8,128)S(1)} copy(bf16[16,16,16,128]{1,0,3,2:T(8,128)(2,1)} %bitcast.81) | data formatting | bytes 3145728 | tf_op jit(solution)/shard_map/vmap()/convert_element_type | solution.py:24
  76.0 3.7 %reshape.191 = f32[256,16,2,64]{3,2,1,0:T(2,128)} reshape(f32[16,16,16,128]{3,2,1,0:T(8,128)S(1)} %bitcast.89) | data formatting | bytes 4194304 | tf_op jit(solution)/shard_map/vmap()/convert_element_type | solution.py:24
  79.7 5.4 %copy.79 = f32[2,256,16,64]{1,3,2,0:T(8,128)S(1)} copy(f32[2,256,16,64]{3,0,2,1:T(2,128)} %bitcast.85) | data formatting | bytes 4194304 | tf_op jit(solution)/shard_map/vmap()/convert_element_type | solution.py:24
  85.1 5.5 %gather_fusion.2 = f32[768,256]{1,0:T(8,128)S(1)} fusion(f32[2,256,1024]{1,2,0:T(8,128)S(1)} %bitcast.82, s32[768]{0:T(1024)S(1)} %reshape.208), kind=kCustom, calls=%fused_computation.2 | custom fusion | bytes 1579008 | tf_op jit(solution)/shard_map/vmap(jit(_take))/gather | solution.py:27
  91.1 1.2 multiply_convert_fusion
  92.8 0.6 fusion.26
  93.4 1.3 collective-permute-start.4
  95.0 2.5 %collective-permute-done.1 = bf16[1,1,256,384]{2,3,1,0:T(8,128)(2,1)S(1)} collective-permute-done((bf16[1,1,256,384]{2,3,1,0:T(8,128)(2,1)S(1)}, bf16[1,1,256,384]{2,3,1,0:T(8,128)(2,1)S(1)}, u32[]{:S(2)}, u32[]{:S(2)}) %collective-permute-start.1) | collective-permute-done | bytes 196640 | tf_op jit(solution)/shard_map/ppermute | solution.py:18
  97.5 1.0 pad_maximum_fusion.1
  98.5 11.1 %collective-permute-start.3 = (bf16[1,4,256,384]{2,3,1,0:T(8,128)(2,1)}, bf16[1,4,256,384]{2,3,1,0:T(8,128)(2,1)}, u32[]{:S(2)}, u32[]{:S(2)}) collective-permute-start(bf16[1,4,256,384]{2,3,1,0:T(8,128)(2,1)} %pad_maximum_fusion.1), channel_id=1, source_target_pairs={{1,0},{2,1},{3,2},{4,3},{5,4},{6,5},{7,6},{8,7},{9,8},{10,9},{11,1... | collective-permute-start | bytes 2359304 | tf_op jit(solution)/shard_map/ppermute | solution.py:18
  109.6 1.9 collective-permute-start.2
  111.5 12.9 %convert_reduce_fusion = f32[16,2048]{0,1:T(8,128)} fusion(bf16[2048,16,16]{2,1,0:T(8,128)(2,1)} %reshape.230), kind=kLoop, calls=%fused_computation.3 | loop fusion | flops 1015808 | bytes 1179648 | tf_op jit(solution)/shard_map/vmap()/reduce_sum | solution.py:25
  124.4 1.3 reduce_sum.45
  125.8 6.7 %collective-permute-start.7 = (bf16[1,4,384]{2,1,0:T(4,128)(2,1)S(1)}, bf16[1,4,384]{2,1,0:T(4,128)(2,1)S(1)}, u32[]{:S(2)}, u32[]{:S(2)}) collective-permute-start(bf16[1,4,384]{2,1,0:T(4,128)(2,1)S(1)} %pad_maximum_fusion.3), channel_id=1, source_target_pairs={{1,0},{2,1},{3,2},{4,3},{5,4},{6,5},{7,6},{8,7},{9,8},{10,9},{11,1... | collective-permute-start | bytes 9224 | tf_op jit(solution)/shard_map/ppermute | solution.py:18
  132.5 2.1 %collective-permute-start.6 = (bf16[1,4,384]{2,1,0:T(4,128)(2,1)S(1)}, bf16[1,4,384]{2,1,0:T(4,128)(2,1)S(1)}, u32[]{:S(2)}, u32[]{:S(2)}) collective-permute-start(bf16[1,4,384]{2,1,0:T(4,128)(2,1)S(1)} %pad_maximum_fusion.3), channel_id=1, source_target_pairs={{0,1},{1,2},{2,3},{3,4},{4,5},{5,6},{6,7},{7,8},{8,9},{9,10},{10,1... | collective-permute-start | bytes 9224 | tf_op jit(solution)/shard_map/ppermute | solution.py:15
  134.6 1.8 copy.82
  136.6 3.5 %collective-permute-done.6 = bf16[1,4,384]{2,1,0:T(4,128)(2,1)S(1)} collective-permute-done((bf16[1,4,384]{2,1,0:T(4,128)(2,1)S(1)}, bf16[1,4,384]{2,1,0:T(4,128)(2,1)S(1)}, u32[]{:S(2)}, u32[]{:S(2)}) %collective-permute-start.6) | collective-permute-done | bytes 3104 | tf_op jit(solution)/shard_map/ppermute | solution.py:15
  140.2 0.6 gather_fusion.1
  140.8 2.7 %pad_maximum_fusion = bf16[3,4,256,384]{2,3,1,0:T(8,128)(2,1)} fusion(bf16[1,4,256,384]{2,3,1,0:T(8,128)(2,1)} %collective-permute-done.3, bf16[1,1,256,384]{2,3,1,0:T(8,128)(2,1)S(1)} %collective-permute-done.1, bf16[1,2,256,384]{2,3,1,0:T(8,128)(2,1)S(1)} %multiply_convert_fusion, bf16[1,1,256,384]{2,3,1,0:T(8,128)(2,1)S(1)} %collective-permute-done, ...), kind=kLoop, calls=%fused_computation.5 | loop fusion | flops 4718592 | bytes 4718592 | tf_op jit(solution)/shard_map/concatenate | solution.py:19
  143.5 3.0 %copy.80 = bf16[3,4,256,384]{3,2,1,0:T(8,128)(2,1)S(1)} copy(bf16[3,4,256,384]{2,3,1,0:T(8,128)(2,1)} %pad_maximum_fusion) | data formatting | bytes 4718592 | tf_op jit(solution)/shard_map/concatenate | solution.py:19
  146.5 2.4 %gather_fusion = bf16[12,256,384]{2,1,0:T(8,128)(2,1)} fusion(bf16[12,256,384]{2,1,0:T(8,128)(2,1)S(1)} %bitcast.86, s32[1024]{0:T(1024)S(1)} %copy-done.7), kind=kCustom, calls=%fused_computation | custom fusion | bytes 4718640 | tf_op jit(solution)/shard_map/gather | solution.py:83
  148.9 3.5 %multiply_reduce_fusion = f32[2,256,256]{2,1,0:T(8,128)S(1)} fusion(bf16[2,6,256,384]{3,2,1,0:T(8,128)(2,1)} %bitcast.87, f32[2,6]{1,0:T(2,128)S(1)} %copy-done.10), kind=kOutput, calls=%fused_computation.4 | convolution fusion | flops 605421568 | bytes 2883632 | tf_op jit(solution)/shard_map/bnko,bnlo->bnkl/dot_general | solution.py:85
  152.7 0.7 fusion.3
  153.4 0.7 fusion.24
  154.2 0.6 fusion.7
  154.8 0.7 fusion.2
  155.5 0.7 fusion.28
  156.1 0.7 fusion.27
  156.8 0.7 fusion.1
  157.5 0.7 fusion.29
  158.1 0.7 fusion.30
  158.8 0.7 fusion.31
  159.6 0.7 fusion
  160.3 0.7 convolution_divide_fusion
  161.5 0.6 fusion.19
  162.1 0.6 add_convert_fusion
  163.3 1.1 copy.86
  164.4 35.3 %all_to_all.30 = bf16[256,16,128]{2,1,0:T(8,128)(2,1)S(1)} all-to-all(bf16[256,16,128]{2,1,0:T(8,128)(2,1)S(1)} %copy.86), channel_id=1, replica_groups=mesh['mem'=16,'reg'=32] {'mem'}, dimensions={0} | all-to-all | bytes 2097152 | tf_op jit(solution)/shard_map/all_to_all | solution.py:106
  199.6 1.3 copy.104
  (64 shorter events, 3.6 us)
Async XLA Ops:
  9.6 21.7 %copy-start.8 = (s32[1,2,5]{2,1,0:T(2,128)S(1)}, s32[1,2,5]{2,1,0:T(2,128)}, u32[]{:S(2)}) copy-start(s32[1,2,5]{2,1,0:T(2,128)} %param.13) | copy-start | bytes 124
  9.6 22.0 %copy-start.4 = (s32[1,2,384]{2,1,0:T(2,128)S(1)}, s32[1,2,384]{2,1,0:T(2,128)}, u32[]{:S(2)}) copy-start(s32[1,2,384]{2,1,0:T(2,128)} %param.11) | copy-start | bytes 9220
  20.9 12.9 %copy-start.5 = (f32[1,2,384]{2,1,0:T(2,128)S(1)}, f32[1,2,384]{2,1,0:T(2,128)}, u32[]{:S(2)}) copy-start(f32[1,2,384]{2,1,0:T(2,128)} %param.10) | copy-start | bytes 9220
  20.9 13.0 %copy-start.12 = (s32[1,2]{1,0:T(1,128)S(1)}, s32[1,2]{1,0:T(1,128)}, u32[]{:S(2)}) copy-start(s32[1,2]{1,0:T(1,128)} %param.12) | copy-start | bytes 28
  20.9 38.4 %all-to-all-start = ((bf16[16,2,16384]{2,1,0:T(2,128)(2,1)}), bf16[16,2,16384]{2,1,0:T(2,128)(2,1)S(1)}, u32[]{:S(2)}, u32[]{:S(2)}) async-start(bf16[16,2,16384]{2,1,0:T(2,128)(2,1)} %reshape.229), calls=%async_computation | async-start | bytes 2097152 | tf_op jit(solution)/shard_map/all_to_all | solution.py:59
  31.5 35.4 %copy-start.9 = (f32[2,6]{1,0:T(2,128)}, f32[2,6]{1,0:T(2,128)S(1)}, u32[]{:S(2)}) copy-start(f32[2,6]{1,0:T(2,128)S(1)} %get-tuple-element.5) | copy-start | bytes 148
  85.1 5.6 %copy-start.6 = (f32[1,2,384]{2,1,0:T(2,128)S(1)}, f32[1,2,384]{2,1,0:T(2,128)}, u32[]{:S(2)}) copy-start(f32[1,2,384]{2,1,0:T(2,128)} %param.9) | copy-start | bytes 9220
  85.1 6.0 %copy-start.11 = (f32[1,2,384]{2,1,0:T(2,128)S(1)}, f32[1,2,384]{2,1,0:T(2,128)}, u32[]{:S(2)}) copy-start(f32[1,2,384]{2,1,0:T(2,128)} %param.8) | copy-start | bytes 9220
  92.3 2.6 %collective-permute-start = (bf16[1,1,256,384]{2,3,1,0:T(8,128)(2,1)S(1)}, bf16[1,1,256,384]{2,3,1,0:T(8,128)(2,1)S(1)}, u32[]{:S(2)}, u32[]{:S(2)}) collective-permute-start(bf16[1,1,256,384]{2,3,1,0:T(8,128)(2,1)S(1)} %get-tuple-element.7), channel_id=1, source_target_pairs={{0,32},{32,64},{64,96},{96,128},{128,160},{160,192},{192,224},{224... | collective-permute-start | bytes 589832 | tf_op jit(solution)/shard_map/ppermute | solution.py:15
  92.4 5.1 %collective-permute-start.1 = (bf16[1,1,256,384]{2,3,1,0:T(8,128)(2,1)S(1)}, bf16[1,1,256,384]{2,3,1,0:T(8,128)(2,1)S(1)}, u32[]{:S(2)}, u32[]{:S(2)}) collective-permute-start(bf16[1,1,256,384]{2,3,1,0:T(8,128)(2,1)S(1)} %get-tuple-element.8), channel_id=1, source_target_pairs={{32,0},{64,32},{96,64},{128,96},{160,128},{192,160},{224,192},{256... | collective-permute-start | bytes 589832 | tf_op jit(solution)/shard_map/ppermute | solution.py:18
  93.4 32.3 %collective-permute-start.4 = (bf16[1,1,384]{2,1,0:T(2,128)(2,1)}, bf16[1,1,384]{2,1,0:T(2,128)(2,1)S(1)}, u32[]{:S(2)}, u32[]{:S(2)}) collective-permute-start(bf16[1,1,384]{2,1,0:T(2,128)(2,1)} %get-tuple-element.9), channel_id=1, source_target_pairs={{0,32},{32,64},{64,96},{96,128},{128,160},{160,192},{192,224},{224... | collective-permute-start | bytes 2312 | tf_op jit(solution)/shard_map/ppermute | solution.py:15
  94.7 31.0 %collective-permute-start.5 = (bf16[1,1,384]{2,1,0:T(2,128)(2,1)}, bf16[1,1,384]{2,1,0:T(2,128)(2,1)S(1)}, u32[]{:S(2)}, u32[]{:S(2)}) collective-permute-start(bf16[1,1,384]{2,1,0:T(2,128)(2,1)} %get-tuple-element.10), channel_id=1, source_target_pairs={{32,0},{64,32},{96,64},{128,96},{160,128},{192,160},{224,192},{256... | collective-permute-start | bytes 2312 | tf_op jit(solution)/shard_map/ppermute | solution.py:18
  98.5 42.3 %collective-permute-start.3 = (bf16[1,4,256,384]{2,3,1,0:T(8,128)(2,1)}, bf16[1,4,256,384]{2,3,1,0:T(8,128)(2,1)}, u32[]{:S(2)}, u32[]{:S(2)}) collective-permute-start(bf16[1,4,256,384]{2,3,1,0:T(8,128)(2,1)} %pad_maximum_fusion.1), channel_id=1, source_target_pairs={{1,0},{2,1},{3,2},{4,3},{5,4},{6,5},{7,6},{8,7},{9,8},{10,9},{11,1... | collective-permute-start | bytes 2359304 | tf_op jit(solution)/shard_map/ppermute | solution.py:18
  109.6 31.2 %collective-permute-start.2 = (bf16[1,4,256,384]{2,3,1,0:T(8,128)(2,1)}, bf16[1,4,256,384]{2,3,1,0:T(8,128)(2,1)}, u32[]{:S(2)}, u32[]{:S(2)}) collective-permute-start(bf16[1,4,256,384]{2,3,1,0:T(8,128)(2,1)} %pad_maximum_fusion.1), channel_id=1, source_target_pairs={{0,1},{1,2},{2,3},{3,4},{4,5},{5,6},{6,7},{7,8},{8,9},{9,10},{10,1... | collective-permute-start | bytes 2359304 | tf_op jit(solution)/shard_map/ppermute | solution.py:15
  125.7 14.5 %copy-start.7 = (s32[1024]{0:T(1024)S(1)}, s32[1024]{0:T(1024)}, u32[]{:S(2)}) copy-start(s32[1024]{0:T(1024)} %pad_clamp_fusion) | copy-start | bytes 12292
  125.8 10.8 %collective-permute-start.7 = (bf16[1,4,384]{2,1,0:T(4,128)(2,1)S(1)}, bf16[1,4,384]{2,1,0:T(4,128)(2,1)S(1)}, u32[]{:S(2)}, u32[]{:S(2)}) collective-permute-start(bf16[1,4,384]{2,1,0:T(4,128)(2,1)S(1)} %pad_maximum_fusion.3), channel_id=1, source_target_pairs={{1,0},{2,1},{3,2},{4,3},{5,4},{6,5},{7,6},{8,7},{9,8},{10,9},{11,1... | collective-permute-start | bytes 9224 | tf_op jit(solution)/shard_map/ppermute | solution.py:18
  132.5 7.7 %collective-permute-start.6 = (bf16[1,4,384]{2,1,0:T(4,128)(2,1)S(1)}, bf16[1,4,384]{2,1,0:T(4,128)(2,1)S(1)}, u32[]{:S(2)}, u32[]{:S(2)}) collective-permute-start(bf16[1,4,384]{2,1,0:T(4,128)(2,1)S(1)} %pad_maximum_fusion.3), channel_id=1, source_target_pairs={{0,1},{1,2},{2,3},{3,4},{4,5},{5,6},{6,7},{7,8},{8,9},{9,10},{10,1... | collective-permute-start | bytes 9224 | tf_op jit(solution)/shard_map/ppermute | solution.py:15
  146.5 2.4 %copy-start.10 = (f32[2,6]{1,0:T(2,128)S(1)}, f32[2,6]{1,0:T(2,128)}, u32[]{:S(2)}) copy-start(f32[2,6]{1,0:T(2,128)} %copy-done.9) | copy-start | bytes 148
  148.9 3.5 %copy-start.3 = (f32[256,256]{1,0:T(8,128)S(1)}, f32[256,256]{1,0:T(8,128)}, u32[]{:S(2)}) copy-start(f32[256,256]{1,0:T(8,128)} %get-tuple-element.11) | copy-start | bytes 786436
  148.9 3.8 %copy-start.2 = (f32[256,256]{1,0:T(8,128)S(1)}, f32[256,256]{1,0:T(8,128)}, u32[]{:S(2)}) copy-start(f32[256,256]{1,0:T(8,128)} %fusion.11) | copy-start | bytes 786436
  156.8 2.0 copy-start
  159.6 2.5 %copy-start.1 = (f32[2,256,1024]{2,1,0:T(8,128)S(1)}, f32[2,256,1024]{2,1,0:T(8,128)}, u32[]{:S(2)}) copy-start(f32[2,256,1024]{2,1,0:T(8,128)} %copy.82) | copy-start | bytes 6291460
where the time goes:
time: 202 us; the launch traced here: 201 us
  local copies, waits for them, and re-layouts  64.1 us (32%)
  blocking collectives  35.3 us (17%)
  starting transfers between devices  34.1 us (17%)
  waiting for transfers between devices  31.1 us (15%)
  other arithmetic  22.8 us (11%)
  matrix products  13.2 us (7%)
    all_to_all x1, blocking collectives, per_device(): lax.all_to_all(regrouped, 'mem', split_axis=0, concat_axis=2, tiled=True)  35.3 us
    unnamed x29, local copies, waits for them, and re-layouts  28.5 us
    all_to_all x1, waiting for transfers between devices, per_device(): lax.all_to_all(background, 'mem', split_axis=2, concat_axis=0, tiled=True)  24.8 us
    convert_element_type x4, local copies, waits for them, and re-layouts, local_obs(): widened = block.astype(jnp.float32)  20 us
    ppermute x4, starting transfers between devices, with_halo(): lax.ppermute(lax.slice_in_dim(block, 0, width, axis=dim), axis, backward)  18.3 us
    reduce_sum x2, other arithmetic, local_obs(): mean_state = jnp.mean(widened, axis=0)  14.2 us
    all_to_all x1, starting transfers between devices, per_device(): lax.all_to_all(background, 'mem', split_axis=2, concat_axis=0, tiled=True)  10.5 us
    gather x2, local copies, waits for them, and re-layouts, local_obs(): predicted = obs_coef * jnp.take(widened, obs_site, axis=1)  5.53 us
  transfers between devices with their start and end apart: 9, of which 4 were waited for; matrix products, arithmetic and copies ran while one was open for 11% of the time, Pallas kernels for 0%

commit v1 on v0

v1 whole, which is shorter than its diff:
```python
import jax
import jax.numpy as jnp
from jax import lax
from jax.experimental import pallas as pl
from jax.experimental.pallas import tpu as pltpu
from jax.sharding import PartitionSpec as P

MESH = pl.DeviceIdType.MESH
F32 = jnp.float32
BF16 = jnp.bfloat16
NS_ITERS = 4
NMEM = 16
NREG = 32
K = 256
OBS = 384
CHUNKS = 8
PACK = 384
MSG = 400
CODE_ROW = 5
SENDS = (8, 7, 9, 6, 10, 5, 11, 4, 12, 3, 13, 2, 14, 1, 15)
EARLY = 5


def split2(x):
    high = x.astype(BF16)
    low = (x - high.astype(F32)).astype(BF16)
    return high, low


def dot(a, b):
    return jnp.dot(a, b, preferred_element_type=F32)


def dot_nt(a, b):
    return lax.dot_general(a, b, (((1,), (1,)), ((), ())), preferred_element_type=F32)


def dot3(a, b):
    return dot(a[0], b[0]) + (dot(a[0], b[1]) + dot(a[1], b[0]))


def rows_of(parts, rows):
    width = parts[0].shape[1]
    index = lax.broadcasted_iota(jnp.int32, (rows, width), 0)
    block = jnp.zeros((rows, width), F32)
    for i, part in enumerate(parts):
        block = jnp.where(index == i, part, block)
    return block


def drive_rows(low_half, high_half):
    a, b = low_half.astype(BF16).astype(F32), high_half.astype(BF16).astype(F32)
    return rows_of([a, b, low_half - a, high_half - b], MSG - PACK).astype(BF16)


def newton_root(matrix):
    n = matrix.shape[0]
    diagonal = lax.broadcasted_iota(jnp.int32, (n, n), 0) == lax.broadcasted_iota(jnp.int32, (n, n), 1)
    eye15 = jnp.where(diagonal, 1.5, 0.0).astype(F32)
    middle = eye15 - 0.5 * matrix
    inverse = split2(middle)
    current = split2(dot3(split2(matrix), inverse))
    for step in range(1, NS_ITERS):
        middle = split2(eye15 - 0.5 * dot3(inverse, current))
        if step < NS_ITERS - 1:
            current = split2(dot3(current, middle))
        product = dot3(middle, inverse)
        inverse = split2(product)
    return product


def kernel(
    x_ref, obs_ref, coef_ref, rinv_ref, site_ref, count_ref, near_ref, out_ref,
    flat, packed, recv, obs_send, obs_recv, code_recv, onehot, own, gmsg, yrecv, center, xsend, xrecv,
    spread, mean, update,
    in_s, in_r, obs_s, obs_r, code_s, code_r, y_s, y_r, x_s, x_r, out_s, out_r, own_s,
):
    me = lax.axis_index("mem")
    reg = lax.axis_index("reg")
    left, right = lax.rem(me + NMEM - 1, NMEM), lax.rem(me + 1, NMEM)
    below, above = lax.rem(reg + NREG - 1, NREG), lax.rem(reg + 1, NREG)
    edge = jnp.logical_or(me == 0, me == NMEM - 1)

    barrier = pltpu.get_barrier_semaphore()
    for i in range(1, NMEM):
        pl.semaphore_signal(
            barrier, inc=1, device_id={"mem": lax.rem(me + i, NMEM)}, device_id_type=MESH
        )
    for side in (below, above):
        pl.semaphore_signal(barrier, inc=1, device_id={"reg": side}, device_id_type=MESH)

    for j in range(2):
        for row, ref in enumerate((obs_ref, coef_ref, rinv_ref)):
            obs_send[j, row : row + 1, :] = ref[0, j : j + 1, :]
        obs_send[j, 3:4, :] = site_ref[0, j : j + 1, :].astype(F32)
        obs_send[j, 4:5, :] = jnp.full((1, OBS), count_ref[0, j].astype(F32))
        for code in range(9):
            value = jnp.float32(1.0 if code == 4 else 0.0)
            taper = 0.5 ** (abs(code // 3 - 1) + abs(code % 3 - 1))
            if code != 4:
                for i in range(5):
                    value = value + jnp.where(near_ref[0, j, i] == code, jnp.float32(taper), jnp.float32(0.0))
            obs_send[j, CODE_ROW + code : CODE_ROW + code + 1, :] = jnp.full((1, OBS), value)

    lane = lax.broadcasted_iota(jnp.int32, (16, 128), 1)
    first = lane < 64

    def reorder(slab, carry):
        columns = pl.ds(pl.multiple_of(slab * 128, 128), 128)
        flat[...] = x_ref[:, :, columns].astype(F32).reshape(256, 128)
        for c in range(CHUNKS):
            even = flat[pl.ds(2 * c, 16, stride=16), :]
            odd = flat[pl.ds(2 * c + 1, 16, stride=16), :]
            packed[2 * slab, c] = jnp.where(first, even, pltpu.roll(odd, 64, 1)).astype(BF16)
            packed[2 * slab + 1, c] = jnp.where(first, pltpu.roll(even, 64, 1), odd).astype(BF16)
        return carry

    lax.fori_loop(0, 16, reorder, 0)
    mine = pl.ds(pl.multiple_of(me * 16, 16), 16)
    for phase in range(2):
        recv[phase, :, mine, :] = packed[phase * NMEM + me]

    pl.semaphore_wait(barrier, NMEM + 1)

    def in_copy(phase, target):
        return pltpu.make_async_remote_copy(
            src_ref=packed.at[phase * NMEM + target],
            dst_ref=recv.at[phase, :, mine, :],
            send_sem=in_s.at[phase, target],
            recv_sem=in_r.at[phase, me],
            device_id={"mem": target},
            device_id_type=MESH,
        )

    def in_wait(phase):
        def one(i, carry):
            source = lax.rem(me + i, NMEM)
            rows = pl.ds(pl.multiple_of(source * 16, 16), 16)
            pltpu.make_async_remote_copy(
                src_ref=packed.at[phase * NMEM + me],
                dst_ref=recv.at[phase, :, rows, :],
                send_sem=in_s.at[phase, me],
                recv_sem=in_r.at[phase, source],
                device_id={"mem": source},
                device_id_type=MESH,
            ).wait_recv()
            return carry

        lax.fori_loop(1, NMEM, one, 0)

    half = me // 8

    def obs_copy(j):
        return pltpu.make_async_remote_copy(
            src_ref=obs_send.at[j],
            dst_ref=obs_recv.at[half],
            send_sem=obs_s.at[j],
            recv_sem=obs_r.at[half],
            device_id={"mem": lax.rem(2 * me + j, NMEM)},
            device_id_type=MESH,
        )

    def obs_far(j):
        return lax.rem(2 * me + j, NMEM) != me

    for j in range(2):
        pl.when(obs_far(j))(lambda j=j: obs_copy(j).start())

        @pl.when(jnp.logical_not(obs_far(j)))
        def _(j=j):
            obs_recv[half] = obs_send[j]

    def second_in(i, wanted):
        target = lax.rem(me + i, NMEM)
        at_edge = jnp.logical_or(target == 0, target == NMEM - 1)
        pl.when(at_edge if wanted else jnp.logical_not(at_edge))(lambda: in_copy(1, target).start())

    for i in SENDS:
        second_in(i, True)
    for i in SENDS:
        in_copy(0, lax.rem(me + i, NMEM)).start()
    for i in SENDS[:EARLY]:
        second_in(i, False)

    def code_copy(phase, side):
        return pltpu.make_async_remote_copy(
            src_ref=obs_recv.at[phase, :, 0:128],
            dst_ref=code_recv.at[phase, side],
            send_sem=code_s.at[phase, side],
            recv_sem=code_r.at[phase, side],
            device_id={"reg": above if side == 0 else below},
            device_id_type=MESH,
        )

    for phase in range(2):
        source = phase * 8 + me // 2

        @pl.when(source != me)
        def _(phase=phase):
            pltpu.make_async_remote_copy(
                src_ref=obs_send.at[0],
                dst_ref=obs_recv.at[phase],
                send_sem=obs_s.at[0],
                recv_sem=obs_r.at[phase],
                device_id={"mem": phase * 8 + me // 2},
                device_id_type=MESH,
            ).wait_recv()

        for side in range(2):
            code_copy(phase, side).start()
        site = obs_recv[phase, 3:4, :].astype(jnp.int32)
        for c in range(CHUNKS):
            place = lax.broadcasted_iota(jnp.int32, (128, OBS), 0) + c * 128
            onehot[phase, c * 128 : (c + 1) * 128, :] = jnp.where(place == site, 1.0, 0.0).astype(BF16)

    def observe(phase):
        values = jnp.concatenate([recv[phase, c] for c in range(CHUNKS)], axis=1)
        predicted = dot(values, onehot[phase]) * obs_recv[phase, 1:2, :]
        mean_pred = jnp.sum(predicted, axis=0, keepdims=True) * (1.0 / K)
        slot = lax.broadcasted_iota(jnp.int32, (1, OBS), 1).astype(F32)
        root = jnp.where(slot < obs_recv[phase, 4:5, :], jnp.sqrt(obs_recv[phase, 2:3, :]), 0.0)
        scaled = (root * (predicted - mean_pred)).astype(BF16)
        misfit = root * (obs_recv[phase, 0:1, :] - mean_pred)
        gram = dot_nt(scaled, scaled)
        a = misfit.astype(BF16).astype(F32)
        b = (misfit - a).astype(BF16).astype(F32)
        parts = rows_of([a, b, misfit - a - b], 16).astype(BF16)
        drive = jnp.sum(dot_nt(parts, scaled), axis=0, keepdims=True)
        for i, block in enumerate((gram[:128, :128], gram[:128, 128:], gram[128:, 128:])):
            own[phase, i * 128 : (i + 1) * 128, :] = block
            gmsg[phase, i * 128 : (i + 1) * 128, :] = block.astype(BF16)
        own[phase, PACK:MSG, :] = rows_of([drive[:, :128], drive[:, 128:]], MSG - PACK)
        gmsg[phase, PACK:MSG, :] = drive_rows(drive[:, :128], drive[:, 128:])

    def y_copy(phase, side):
        wraps = me == (NMEM - 1 if side == 0 else 0)
        return pltpu.make_async_remote_copy(
            src_ref=gmsg.at[jnp.where(wraps, 1 - phase, phase)],
            dst_ref=yrecv.at[phase, side],
            send_sem=y_s.at[phase, side],
            recv_sem=y_r.at[phase, side],
            device_id={"mem": right if side == 0 else left},
            device_id_type=MESH,
        )

    def x_copy(phase, side):
        return pltpu.make_async_remote_copy(
            src_ref=xsend.at[phase, side],
            dst_ref=xrecv.at[phase, side],
            send_sem=x_s.at[phase, side],
            recv_sem=x_r.at[phase, side],
            device_id={"reg": above if side == 0 else below},
            device_id_type=MESH,
        )

    def center_state(phase):
        for c in range(CHUNKS):
            values = recv[phase, c].astype(F32)
            average = jnp.sum(values, axis=0, keepdims=True) * (1.0 / K)
            mean[phase, :, c * 128 : (c + 1) * 128] = jnp.broadcast_to(average, (8, 128))
            spread[phase, :, c * 128 : (c + 1) * 128] = (values - average).astype(BF16)

    def sum_row(phase):
        for side in range(2):
            y_copy(phase, side).wait_recv()
            code_copy(phase, side).wait_recv()

        def weighted(weights, first_code, rows):
            w = [weights[CODE_ROW + first_code + i : CODE_ROW + first_code + i + 1, :] for i in range(3)]
            return (
                w[0] * yrecv[phase, 0, rows, :].astype(F32)
                + w[1] * own[phase, rows, :]
                + w[2] * yrecv[phase, 1, rows, :].astype(F32)
            )

        for side in range(2):
            weights = code_recv[phase, 1 - side]
            first_code = 0 if side == 0 else 6
            for i in range(3):
                rows = slice(i * 128, (i + 1) * 128)
                xsend[phase, side, rows, :] = weighted(weights, first_code, rows).astype(BF16)
            tail = weighted(weights, first_code, slice(PACK, MSG))
            xsend[phase, side, PACK:MSG, :] = drive_rows(
                tail[0:1] + tail[2:3], tail[1:2] + tail[3:4]
            )
            x_copy(phase, side).start()
        center[phase] = weighted(obs_recv[phase, :, 0:128], 3, slice(0, MSG))

    def transform(phase):
        for side in range(2):
            x_copy(phase, side).wait_recv()
        total = center[phase] + xrecv[phase, 0].astype(F32) + xrecv[phase, 1].astype(F32)
        tail = total[PACK:MSG]
        drive = jnp.concatenate([tail[0:1] + tail[2:3], tail[1:2] + tail[3:4]], axis=1)
        corner = total[128:256]
        system = jnp.concatenate(
            [
                jnp.concatenate([total[0:128], corner], axis=1),
                jnp.concatenate([corner.T, total[256:384]], axis=1),
            ],
            axis=0,
        )
        diagonal = lax.broadcasted_iota(jnp.int32, (K, K), 0) == lax.broadcasted_iota(jnp.int32, (K, K), 1)
        system = system + jnp.where(diagonal, K - 1.0, 0.0)
        scale = jnp.max(jnp.sum(jnp.abs(system), axis=0, keepdims=True), axis=1, keepdims=True)
        half = newton_root(system / scale) / jnp.sqrt(scale)
        halves = split2(half)
        vector = jnp.broadcast_to(drive, (16, K))
        vector = dot3(split2(vector), halves)
        vector = dot3(split2(vector), halves)[0:1]
        return (jnp.float32(K - 1.0) ** 0.5 * half + vector).astype(BF16)

    def apply(phase, weights):
        for c in range(0, CHUNKS, 2):
            columns = slice(c * 128, (c + 2) * 128)
            result = dot(weights, spread[phase, :, columns]) + mean[phase, 0:1, columns]
            update[phase, c] = result[:, :128].astype(BF16)
            update[phase, c + 1] = result[:, 128:].astype(BF16)

    def out_copy(phase, target):
        rows = pl.ds(pl.multiple_of(target * 16, 16), 16)
        return pltpu.make_async_remote_copy(
            src_ref=update.at[phase, :, rows, :],
            dst_ref=out_ref.at[phase, me],
            send_sem=out_s.at[phase, target],
            recv_sem=out_r.at[phase, me],
            device_id={"mem": target},
            device_id_type=MESH,
        )

    def own_copy(phase):
        return pltpu.make_async_copy(update.at[phase, :, mine, :], out_ref.at[phase, me], own_s.at[phase])

    def send_out(phase):
        for i in SENDS:
            out_copy(phase, lax.rem(me + i, NMEM)).start()
        own_copy(phase).start()

    in_wait(0)
    observe(0)

    @pl.when(edge)
    def _():
        in_wait(1)
        observe(1)

    for side in range(2):
        y_copy(0, side).start()
    for i in SENDS[EARLY:]:
        second_in(i, False)
    center_state(0)
    sum_row(0)

    @pl.when(jnp.logical_not(edge))
    def _():
        in_wait(1)
        observe(1)

    for side in range(2):
        y_copy(1, side).start()
    center_state(1)
    apply(0, transform(0))
    send_out(0)
    sum_row(1)
    apply(1, transform(1))
    send_out(1)

    for phase in range(2):
        own_copy(phase).wait()

        def finish(i, carry, phase=phase):
            other = lax.rem(me + i, NMEM)
            in_copy(phase, other).wait_send()
            out_copy(phase, other).wait_send()
            pltpu.make_async_remote_copy(
                src_ref=update.at[phase, :, mine, :],
                dst_ref=out_ref.at[phase, other],
                send_sem=out_s.at[phase, me],
                recv_sem=out_r.at[phase, other],
                device_id={"mem": other},
                device_id_type=MESH,
            ).wait_recv()
            return carry

        lax.fori_loop(1, NMEM, finish, 0)
        for side in range(2):
            code_copy(phase, side).wait_send()
            y_copy(phase, side).wait_send()
            x_copy(phase, side).wait_send()
    for j in range(2):
        pl.when(obs_far(j))(lambda j=j: obs_copy(j).wait_send())


def order_back(in_ref, out_ref, flat):
    first = lax.broadcasted_iota(jnp.int32, (16, 128), 1) < 64
    for p in range(in_ref.shape[0] // 2):
        for c in range(CHUNKS):
            a = in_ref[2 * p, c].astype(F32)
            b = in_ref[2 * p + 1, c].astype(F32)
            flat[p, pl.ds(2 * c, 16, stride=16), :] = jnp.where(first, a, pltpu.roll(b, 64, 1))
            flat[p, pl.ds(2 * c + 1, 16, stride=16), :] = jnp.where(first, pltpu.roll(a, 64, 1), b)
        out_ref[:, :, p * 128 : (p + 1) * 128] = flat[p].reshape(16, 16, 128).astype(BF16)


def per_device(background, observations, obs_coef, obs_rinv, obs_site, obs_count, neighbours):
    vmem = pl.BlockSpec(memory_space=pltpu.VMEM)
    smem = pl.BlockSpec(memory_space=pltpu.SMEM)
    dma = pltpu.SemaphoreType.DMA
    moved = pl.pallas_call(
        kernel,
        out_shape=jax.ShapeDtypeStruct((2, NMEM, CHUNKS, 16, 128), BF16),
        in_specs=[vmem] * 5 + [smem] * 2,
        out_specs=pl.BlockSpec(memory_space=pl.ANY),
        scratch_shapes=[
            pltpu.VMEM((256, 128), F32),
            pltpu.VMEM((2 * NMEM, CHUNKS, 16, 128), BF16),
            pltpu.VMEM((2, CHUNKS, K, 128), BF16),
            pltpu.VMEM((2, 16, OBS), F32),
            pltpu.VMEM((2, 16, OBS), F32),
            pltpu.VMEM((2, 2, 16, 128), F32),
            pltpu.VMEM((2, CHUNKS * 128, OBS), BF16),
            pltpu.VMEM((2, MSG, 128), F32),
            pltpu.VMEM((2, MSG, 128), BF16),
            pltpu.VMEM((2, 2, MSG, 128), BF16),
            pltpu.VMEM((2, MSG, 128), F32),
            pltpu.VMEM((2, 2, MSG, 128), BF16),
            pltpu.VMEM((2, 2, MSG, 128), BF16),
            pltpu.VMEM((2, K, CHUNKS * 128), BF16),
            pltpu.VMEM((2, 8, CHUNKS * 128), F32),
            pltpu.VMEM((2, CHUNKS, K, 128), BF16),
            dma((2, NMEM)), dma((2, NMEM)),
            dma((2,)), dma((2,)),
            dma((2, 2)), dma((2, 2)),
            dma((2, 2)), dma((2, 2)),
            dma((2, 2)), dma((2, 2)),
            dma((2, NMEM)), dma((2, NMEM)),
            dma((2,)),
        ],
        compiler_params=pltpu.CompilerParams(
            collective_id=0, has_side_effects=True, vmem_limit_bytes=40 << 20
        ),
        name="analysis",
    )(background, observations, obs_coef, obs_rinv, obs_site, obs_count, neighbours)
    steps = 4
    blocks = 2 * NMEM // steps
    width = background.shape[2] // steps
    return pl.pallas_call(
        order_back,
        grid=(steps,),
        out_shape=jax.ShapeDtypeStruct(background.shape, BF16),
        in_specs=[pl.BlockSpec((blocks, CHUNKS, 16, 128), lambda i: (i, 0, 0, 0))],
        out_specs=pl.BlockSpec((16, 16, width), lambda i: (0, 0, i)),
        scratch_shapes=[pltpu.VMEM((blocks // 2, 256, 128), F32)],
        name="order_back",
    )(moved.reshape(2 * NMEM, CHUNKS, 16, 128))


def solution(mesh):
    in_specs = (
        P("mem", None, "reg"),
        P("reg", "mem", None),
        P("reg", "mem", None),
        P("reg", "mem", None),
        P("reg", "mem", None),
        P("reg", "mem"),
        P("reg", "mem", None),
    )
    out_specs = P("mem", None, "reg")
    return jax.shard_map(
        per_device, mesh=mesh, in_specs=in_specs, out_specs=out_specs, check_vma=False
    )
```

time: 202 us -> 85.2 us (0.42)
  Pallas kernels: 0 us -> 78.5 us
  local copies, waits for them, and re-layouts: 64.1 us -> 6.25 us
  blocking collectives: 35.3 us -> 0 us
  starting transfers between devices: 34.1 us -> 0 us
  waiting for transfers between devices: 31.1 us -> 0 us
  other arithmetic: 22.8 us -> 0 us
  matrix products: 13.2 us -> 0 us
    pallas_call x0 -> x2, Pallas kernels: none -> 78.5 us  [the longest x1 74.6 us: per_device(): pl.pallas_call(kernel, out_shape=jax.ShapeDtypeStruct((2, NMEM, CHUNKS, 1...]
    all_to_all x1 -> x0, blocking collectives: 35.3 us -> none  [per_device(): lax.all_to_all(regrouped, 'mem', split_axis=0, concat_axis=2, tiled=True)]
    all_to_all x1 -> x0, waiting for transfers between devices: 24.8 us -> none  [per_device(): lax.all_to_all(background, 'mem', split_axis=2, concat_axis=0, tiled=True)]
    ppermute x8 -> x0, starting transfers between devices: 23.6 us -> none  [the longest x4 18.3 us: with_halo(): lax.ppermute(lax.slice_in_dim(block, 0, width, axis=dim), axis, backward)]
    unnamed x29 -> x16, local copies, waits for them, and re-layouts: 28.5 us -> 6.25 us
    convert_element_type x5 -> x0, local copies, waits for them, and re-layouts: 20.5 us -> none  [the longest x4 20 us: local_obs(): widened = block.astype(jnp.float32)]
    reduce_sum x5 -> x0, other arithmetic: 14.8 us -> none  [the longest x2 14.2 us: local_obs(): mean_state = jnp.mean(widened, axis=0)]
    dot_general x16 -> x0, matrix products: 13.2 us -> none  [the longest x1 3.47 us: per_device(): jnp.einsum('bnko,bnlo->bnkl', near_scaled, near_scaled, preferred_element...]
  transfers between devices with their start and end apart: 9 -> 0, of which waited for: 4 -> 0; matrix products, arithmetic and copies ran while one was open for 11% -> 0% of each run, Pallas kernels for 0% -> 0%
where the time goes in v1:
time: 85.2 us; the launch traced here: 84.8 us
  Pallas kernels  78.5 us (92%)
  local copies, waits for them, and re-layouts  6.25 us (7%)
    pallas_call x1, Pallas kernels, per_device(): pl.pallas_call(kernel, out_shape=jax.ShapeDtypeStruct((2, NMEM, CHUNKS, 1...  74.6 us
    unnamed x16, local copies, waits for them, and re-layouts  6.25 us
    pallas_call x1, Pallas kernels, per_device(): pl.pallas_call(order_back, grid=(steps,), out_shape=jax.ShapeDtypeStruct(...  3.9 us

profile of v1, /device:TPU:1, one launch (start us, length us, event | category | flops | bytes accessed | tf_op | source)
XLA Modules:
  0.0 84.8 jit_solution(9128258091809714660)
XLA Ops:
  0.0 0.0 copy-start.1
  0.0 1.2 %copy-done.1 = bf16[16,16,2048]{2,1,0:T(8,128)(2,1)S(1)} copy-done((bf16[16,16,2048]{2,1,0:T(8,128)(2,1)S(1)}, bf16[16,16,2048]{2,1,0:T(8,128)(2,1)}, u32[]{:S(2)}) %copy-start.1) | copy-done | bytes 1048600
  1.2 0.0 copy-start.2
  1.2 0.7 copy-done.2
  1.9 0.0 copy-start.3
  1.9 0.7 copy-done.3
  2.6 0.0 copy-start.4
  2.6 0.7 copy-done.4
  3.3 0.0 copy-start.5
  3.3 0.7 copy-done.5
  4.0 0.0 copy-start.6
  4.0 0.7 copy-done.6
  4.6 0.0 copy-start.7
  4.6 0.7 copy-done.7
  5.3 74.6 %analysis.1 = bf16[2,16,8,16,128]{4,3,2,1,0:T(8,128)(2,1)S(1)} custom-call(bf16[16,16,2048]{2,1,0:T(8,128)(2,1)S(1)} %copy-done.1, f32[1,2,384]{2,1,0:T(2,128)S(1)} %copy-done.2, f32[1,2,384]{2,1,0:T(2,128)S(1)} %copy-done.3, f32[1,2,384]{2,1,0:T(2,128)S(1)} %copy-done.4, s32[1,2,384]{2,1,0:T(2,128)S(1)} %copy-done.5, s32[1,2]{1,0:T(1,128)S(1)} %copy-done.7, ...), custom_call_target="tpu_custom_call" | custom-call | tf_op jit(solution)/shard_map/analysis/pallas_call | solution.py:409
  80.0 0.0 copy-start
  80.0 1.0 %copy-done = bf16[2,16,8,16,128]{4,3,2,1,0:T(8,128)(2,1)} copy-done((bf16[2,16,8,16,128]{4,3,2,1,0:T(8,128)(2,1)}, bf16[2,16,8,16,128]{4,3,2,1,0:T(8,128)(2,1)S(1)}, u32[]{:S(2)}) %copy-start) | copy-done | bytes 1048600
  80.9 3.9 %order_back.1 = bf16[16,16,2048]{2,1,0:T(8,128)(2,1)} custom-call(bf16[32,8,16,128]{3,2,1,0:T(8,128)(2,1)} %bitcast.1), custom_call_target="tpu_custom_call" | custom-call | tf_op jit(solution)/shard_map/order_back/pallas_call | solution.py:447
Async XLA Ops:
  0.0 1.2 %copy-start.1 = (bf16[16,16,2048]{2,1,0:T(8,128)(2,1)S(1)}, bf16[16,16,2048]{2,1,0:T(8,128)(2,1)}, u32[]{:S(2)}) copy-start(bf16[16,16,2048]{2,1,0:T(8,128)(2,1)} %x_ref.1) | copy-start | bytes 3145732
  1.2 0.7 copy-start.2
  1.9 0.7 copy-start.3
  2.6 0.7 copy-start.4
  3.3 0.7 copy-start.5
  4.0 0.7 copy-start.6
  4.6 0.7 copy-start.7
  80.0 1.0 %copy-start = (bf16[2,16,8,16,128]{4,3,2,1,0:T(8,128)(2,1)}, bf16[2,16,8,16,128]{4,3,2,1,0:T(8,128)(2,1)S(1)}, u32[]{:S(2)}) copy-start(bf16[2,16,8,16,128]{4,3,2,1,0:T(8,128)(2,1)S(1)} %analysis.1) | copy-start | bytes 3145732

commit v2 on v1

v2 whole, which is shorter than its diff:
```python
import contextlib

import jax
import jax.numpy as jnp
from jax import lax
from jax.experimental import pallas as pl
from jax.experimental.pallas import tpu as pltpu
from jax.sharding import PartitionSpec as P

MESH = pl.DeviceIdType.MESH
F32 = jnp.float32
BF16 = jnp.bfloat16
NS_ITERS = 4
NMEM = 16
NREG = 32
K = 256
OBS = 384
CHUNKS = 8
PACK = 384
MSG = 400
PARTS = ((0, 128), (128, 256), (256, MSG))
CODE_ROW = 5
SENDS = tuple((away, core) for away in (3, 2, 1, 4, -3, -2, -1) for core in range(2)) + ((0, 0),)
EARLY = 6
EARLY_OUT = 6


def split2(x):
    high = x.astype(BF16)
    low = (x - high.astype(F32)).astype(BF16)
    return high, low


def dot(a, b):
    return jnp.dot(a, b, preferred_element_type=F32)


def dot_nt(a, b):
    return lax.dot_general(a, b, (((1,), (1,)), ((), ())), preferred_element_type=F32)


def dot3(a, b):
    return dot(a[0], b[0]) + (dot(a[0], b[1]) + dot(a[1], b[0]))


def rows_of(parts, rows):
    width = parts[0].shape[1]
    index = lax.broadcasted_iota(jnp.int32, (rows, width), 0)
    block = jnp.zeros((rows, width), F32)
    for i, part in enumerate(parts):
        block = jnp.where(index == i, part, block)
    return block


def drive_rows(low_half, high_half):
    a, b = low_half.astype(BF16).astype(F32), high_half.astype(BF16).astype(F32)
    return rows_of([a, b, low_half - a, high_half - b], MSG - PACK).astype(BF16)


def newton_root(matrix):
    n = matrix.shape[0]
    diagonal = lax.broadcasted_iota(jnp.int32, (n, n), 0) == lax.broadcasted_iota(jnp.int32, (n, n), 1)
    eye15 = jnp.where(diagonal, 1.5, 0.0).astype(F32)
    middle = eye15 - 0.5 * matrix
    inverse = split2(middle)
    current = split2(dot3(split2(matrix), inverse))
    for step in range(1, NS_ITERS):
        middle = split2(eye15 - 0.5 * dot3(inverse, current))
        if step < NS_ITERS - 1:
            current = split2(dot3(current, middle))
        product = dot3(middle, inverse)
        inverse = split2(product)
    return product


def stage(name):
    return contextlib.nullcontext()


def kernel(
    x_hbm, obs_hbm, coef_hbm, rinv_hbm, site_hbm, count_hbm, near_hbm, out_hbm,
    state, obs_in, coef_in, rinv_in, site_in, count_in, near_in,
    flat, packed, recv, obs_send, obs_recv, code_recv, onehot, own, gmsg, yrecv, center, xsend, xrecv,
    spread, mean, update, returned, ordered,
    region_in, adjacent_in, state_s, small_s, in_s, in_r, obs_s, obs_r, code_s, code_r, y_s, y_r, x_s, x_r, out_s, out_r, result_s,
):
    me = lax.axis_index("mem")
    reg = lax.axis_index("reg")
    chip = me // 2
    left, right = lax.rem(me + NMEM - 1, NMEM), lax.rem(me + 1, NMEM)
    below, above = lax.rem(reg + NREG - 1, NREG), lax.rem(reg + 1, NREG)
    edge = jnp.logical_or(me == 0, me == NMEM - 1)

    core = lax.rem(me, 2)
    sibling = me + 1 - 2 * core
    barrier = pltpu.get_barrier_semaphore()

    def greet(target):
        pl.semaphore_signal(barrier, inc=1, device_id={"mem": target}, device_id_type=MESH)

    pl.when(core == 1)(lambda: greet(sibling))
    for i in range(1, 8):
        greet(2 * lax.rem(chip + i, 8))
    for side in (below, above):
        pl.semaphore_signal(
            barrier, inc=1, device_id={"mem": 2 * chip + 1, "reg": side}, device_id_type=MESH
        )

    def pass_barrier(hearer, count, passed):
        @pl.when(core == hearer)
        def _():
            pl.semaphore_wait(barrier, count)
            pl.semaphore_signal(passed, inc=1, device_id={"mem": sibling}, device_id_type=MESH)

        pl.when(core != hearer)(lambda: pl.semaphore_wait(passed, 1))

    def slab_of(step):
        away = 4 + lax.div(step + 1, 2) * (1 - 2 * lax.rem(step, 2))
        return lax.rem(chip + away, 8)

    def lanes(slab):
        return pl.ds(pl.multiple_of(slab * 128, 128), 128)

    def state_copy(phase):
        columns = pl.ds(phase * 1024, 1024)
        return pltpu.make_async_copy(
            x_hbm.at[:, :, columns], state.at[:, :, columns], state_s.at[phase]
        )

    small = [
        pltpu.make_async_copy(source, target, small_s.at[i])
        for i, (source, target) in enumerate(
            (
                (obs_hbm, obs_in), (coef_hbm, coef_in), (rinv_hbm, rinv_in), (site_hbm, site_in),
                (count_hbm, count_in), (near_hbm, near_in),
            )
        )
    ]

    state_copy(0).start()
    for copy in small:
        copy.start()
    state_copy(1).start()

    first = lax.broadcasted_iota(jnp.int32, (16, 128), 1) < 64
    mine = pl.ds(pl.multiple_of(me * 16, 16), 16)

    def reorder(slab):
        flat[...] = state[:, :, lanes(slab)].astype(F32).reshape(256, 128)
        for c in range(CHUNKS):
            even = flat[pl.ds(2 * c, 16, stride=16), :]
            odd = flat[pl.ds(2 * c + 1, 16, stride=16), :]
            packed[2 * slab, c] = jnp.where(first, even, pltpu.roll(odd, 64, 1)).astype(BF16)
            packed[2 * slab + 1, c] = jnp.where(first, pltpu.roll(even, 64, 1), odd).astype(BF16)

    def in_copy(phase, target):
        return pltpu.make_async_remote_copy(
            src_ref=packed.at[phase * NMEM + target],
            dst_ref=recv.at[phase, :, mine, :],
            send_sem=in_s.at[phase],
            recv_sem=in_r.at[phase],
            device_id={"mem": target},
            device_id_type=MESH,
        )

    def in_all(phase):
        others = recv.at[phase, :, pl.ds(0, K - 16), :]
        return pltpu.make_async_remote_copy(
            src_ref=others,
            dst_ref=others,
            send_sem=in_s.at[phase],
            recv_sem=in_r.at[phase],
            device_id={"mem": sibling},
            device_id_type=MESH,
        )

    def in_wait(phase):
        in_all(phase).wait_recv()

    half = me // 8

    def obs_copy(j):
        return pltpu.make_async_remote_copy(
            src_ref=obs_send.at[j],
            dst_ref=obs_recv.at[half],
            send_sem=obs_s.at[j],
            recv_sem=obs_r.at[half],
            device_id={"mem": lax.rem(2 * me + j, NMEM)},
            device_id_type=MESH,
        )

    def obs_far(j):
        return lax.rem(2 * me + j, NMEM) != me

    def first_in(step, carry):
        slab = slab_of(step)
        reorder(slab)
        for core in range(2):
            target = 2 * slab + core
            pl.when(target != me)(lambda target=target: in_copy(0, target).start())
        return carry

    with stage("barrier"):
        state_copy(0).wait()
        pass_barrier(0, NMEM - 1, region_in)
    with stage("first_in_a"):
        lax.fori_loop(0, 2, first_in, 0)

    with stage("obs_send"):
        for copy in small:
            copy.wait()
        row = lax.broadcasted_iota(jnp.int32, (16, OBS), 0)
        code = row - CODE_ROW
        away = jnp.abs(code // 3 - 1) + jnp.abs(lax.rem(code + 15, 3) - 1)
        taper = jnp.where(away == 0, 1.0, jnp.where(away == 1, 0.5, 0.25))
        for j in range(2):
            block = jnp.where(code == 4, 1.0, 0.0)
            for i in range(5):
                block = block + jnp.where(code == near_in[0, j : j + 1, i : i + 1], taper, 0.0)
            count = jnp.broadcast_to(count_in[0:1, j : j + 1].astype(F32), (16, OBS))
            obs_send[j] = jnp.where(row == 4, count, block)
            for i, ref in enumerate((obs_in, coef_in, rinv_in)):
                obs_send[j, i : i + 1, :] = ref[0, j : j + 1, :]
            obs_send[j, 3:4, :] = site_in[0, j : j + 1, :].astype(F32)
        for j in range(2):
            pl.when(obs_far(j))(lambda j=j: obs_copy(j).start())

            @pl.when(jnp.logical_not(obs_far(j)))
            def _(j=j):
                obs_recv[half] = obs_send[j]

    def partner(away, core):
        if away == 0:
            return 2 * chip + 1 - lax.rem(me, 2)
        turned = away * (1 - 2 * lax.rem(me, 2))
        return 2 * lax.rem(chip + 8 + turned, 8) + core

    def second_in(i, wanted):
        target = partner(*i)
        at_edge = jnp.logical_or(target == 0, target == NMEM - 1)
        pl.when(at_edge if wanted else jnp.logical_not(at_edge))(lambda: in_copy(1, target).start())

    def reorder_step(slab, carry):
        reorder(slab)
        return carry

    with stage("first_in_b"):
        lax.fori_loop(2, 8, first_in, 0)
    with stage("second_in"):
        state_copy(1).wait()
        reorder(8)
        reorder(15)
        for i in SENDS:
            second_in(i, True)
        lax.fori_loop(9, 15, reorder_step, 0)
        for i in SENDS[:EARLY]:
            second_in(i, False)
        recv[0, :, mine, :] = packed[me]
        recv[1, :, mine, :] = packed[NMEM + me]

    def code_copy(phase, side):
        return pltpu.make_async_remote_copy(
            src_ref=obs_recv.at[phase, :, 0:128],
            dst_ref=code_recv.at[phase, side],
            send_sem=code_s,
            recv_sem=code_r,
            device_id={"reg": above if side == 0 else below},
            device_id_type=MESH,
        )

    def codes_all():
        return pltpu.make_async_remote_copy(
            src_ref=code_recv,
            dst_ref=code_recv,
            send_sem=code_s,
            recv_sem=code_r,
            device_id={"reg": above},
            device_id_type=MESH,
        )

    with stage("onehot"):
        for phase in range(2):
            @pl.when(phase * 8 + chip != me)
            def _(phase=phase):
                pltpu.make_async_remote_copy(
                    src_ref=obs_send.at[0],
                    dst_ref=obs_recv.at[phase],
                    send_sem=obs_s.at[0],
                    recv_sem=obs_r.at[phase],
                    device_id={"mem": phase * 8 + chip},
                    device_id_type=MESH,
                ).wait_recv()

            site = obs_recv[phase, 3:4, :].astype(jnp.int32)
            for c in range(CHUNKS):
                place = lax.broadcasted_iota(jnp.int32, (128, OBS), 0) + c * 128
                onehot[phase, c * 128 : (c + 1) * 128, :] = jnp.where(place == site, 1.0, 0.0).astype(BF16)

    def observe(phase):
        values = jnp.concatenate([recv[phase, c] for c in range(CHUNKS)], axis=1)
        predicted = dot(values, onehot[phase]) * obs_recv[phase, 1:2, :]
        mean_pred = jnp.sum(predicted, axis=0, keepdims=True) * (1.0 / K)
        slot = lax.broadcasted_iota(jnp.int32, (1, OBS), 1).astype(F32)
        root = jnp.where(slot < obs_recv[phase, 4:5, :], jnp.sqrt(obs_recv[phase, 2:3, :]), 0.0)
        scaled = (root * (predicted - mean_pred)).astype(BF16)
        misfit = root * (obs_recv[phase, 0:1, :] - mean_pred)
        gram = dot_nt(scaled, scaled)
        a = misfit.astype(BF16).astype(F32)
        b = (misfit - a).astype(BF16).astype(F32)
        parts = rows_of([a, b, misfit - a - b], 16).astype(BF16)
        drive = jnp.sum(dot_nt(parts, scaled), axis=0, keepdims=True)
        for i, block in enumerate((gram[:128, :128], gram[:128, 128:], gram[128:, 128:])):
            own[phase, i * 128 : (i + 1) * 128, :] = block
            gmsg[phase, i * 128 : (i + 1) * 128, :] = block.astype(BF16)
        own[phase, PACK:MSG, :] = rows_of([drive[:, :128], drive[:, 128:]], MSG - PACK)
        gmsg[phase, PACK:MSG, :] = drive_rows(drive[:, :128], drive[:, 128:])

    def y_wraps(side):
        return me == (NMEM - 1 if side == 0 else 0)

    def y_copy(phase, side, part):
        rows = slice(*PARTS[part])
        return pltpu.make_async_remote_copy(
            src_ref=gmsg.at[jnp.where(y_wraps(side), 1 - phase, phase), rows],
            dst_ref=yrecv.at[phase, side, rows],
            send_sem=y_s.at[phase],
            recv_sem=y_r.at[phase, part],
            device_id={"mem": right if side == 0 else left},
            device_id_type=MESH,
        )

    def y_start(phase, side):
        for part in range(len(PARTS)):
            y_copy(phase, side, part).start()

    def x_copy(phase, side, part):
        rows = slice(*PARTS[part])
        return pltpu.make_async_remote_copy(
            src_ref=xsend.at[phase, side, rows],
            dst_ref=xrecv.at[phase, side, rows],
            send_sem=x_s.at[phase],
            recv_sem=x_r.at[phase],
            device_id={"reg": above if side == 0 else below},
            device_id_type=MESH,
        )

    def y_all(phase, rows, part=0):
        both = yrecv.at[phase, :, rows]
        return pltpu.make_async_remote_copy(
            src_ref=both,
            dst_ref=both,
            send_sem=y_s.at[phase],
            recv_sem=y_r.at[phase, part],
            device_id={"mem": sibling},
            device_id_type=MESH,
        )

    def x_all(phase):
        return pltpu.make_async_remote_copy(
            src_ref=xsend.at[phase],
            dst_ref=xrecv.at[phase],
            send_sem=x_s.at[phase],
            recv_sem=x_r.at[phase],
            device_id={"reg": above},
            device_id_type=MESH,
        )

    def x_wait(phase):
        x_all(phase).wait_recv()

    def center_state(phase):
        for c in range(CHUNKS):
            values = recv[phase, c].astype(F32)
            average = jnp.sum(values, axis=0, keepdims=True) * (1.0 / K)
            mean[phase, :, c * 128 : (c + 1) * 128] = jnp.broadcast_to(average, (8, 128))
            spread[phase, :, c * 128 : (c + 1) * 128] = (values - average).astype(BF16)

    def sum_row(phase):
        def weighted(weights, first_code, rows):
            w = [weights[CODE_ROW + first_code + i : CODE_ROW + first_code + i + 1, :] for i in range(3)]
            return (
                w[0] * yrecv[phase, 0, rows, :].astype(F32)
                + w[1] * own[phase, rows, :]
                + w[2] * yrecv[phase, 1, rows, :].astype(F32)
            )

        for part in range(len(PARTS)):
            rows = slice(part * 128, (part + 1) * 128)
            y_all(phase, slice(*PARTS[part]), part).wait_recv()
            for side in range(2):
                weights = code_recv[phase, 1 - side]
                first_code = 0 if side == 0 else 6
                xsend[phase, side, rows, :] = weighted(weights, first_code, rows).astype(BF16)
                if part == len(PARTS) - 1:
                    tail = weighted(weights, first_code, slice(PACK, MSG))
                    xsend[phase, side, PACK:MSG, :] = drive_rows(
                        tail[0:1] + tail[2:3], tail[1:2] + tail[3:4]
                    )
                x_copy(phase, side, part).start()
        center[phase] = weighted(obs_recv[phase, :, 0:128], 3, slice(0, MSG))

    def transform(phase):
        total = center[phase] + xrecv[phase, 0].astype(F32) + xrecv[phase, 1].astype(F32)
        tail = total[PACK:MSG]
        drive = jnp.concatenate([tail[0:1] + tail[2:3], tail[1:2] + tail[3:4]], axis=1)
        corner = total[128:256]
        system = jnp.concatenate(
            [
                jnp.concatenate([total[0:128], corner], axis=1),
                jnp.concatenate([corner.T, total[256:384]], axis=1),
            ],
            axis=0,
        )
        diagonal = lax.broadcasted_iota(jnp.int32, (K, K), 0) == lax.broadcasted_iota(jnp.int32, (K, K), 1)
        system = system + jnp.where(diagonal, K - 1.0, 0.0)
        scale = jnp.max(jnp.sum(jnp.abs(system), axis=0, keepdims=True), axis=1, keepdims=True)
        half_root = newton_root(system / scale) / jnp.sqrt(scale)
        halves = split2(half_root)
        vector = jnp.broadcast_to(drive, (16, K))
        vector = dot3(split2(vector), halves)
        vector = dot3(split2(vector), halves)[0:1]
        return (jnp.float32(K - 1.0) ** 0.5 * half_root + vector).astype(BF16)

    def apply(phase, weights):
        for c in range(0, CHUNKS, 2):
            columns = slice(c * 128, (c + 2) * 128)
            result = dot(weights, spread[phase, :, columns]) + mean[phase, 0:1, columns]
            update[phase, c] = result[:, :128].astype(BF16)
            update[phase, c + 1] = result[:, 128:].astype(BF16)

    def out_copy(phase, target):
        rows = pl.ds(pl.multiple_of(target * 16, 16), 16)
        return pltpu.make_async_remote_copy(
            src_ref=update.at[phase, :, rows, :],
            dst_ref=returned.at[phase, me],
            send_sem=out_s.at[phase],
            recv_sem=out_r.at[phase, chip],
            device_id={"mem": target},
            device_id_type=MESH,
        )

    def send_out(phase, offsets):
        for i in offsets:
            out_copy(phase, partner(*i)).start()

    def keep_own(phase):
        returned[phase, me] = update[phase, :, mine, :]

    def result_copy(slab):
        return pltpu.make_async_copy(
            ordered.at[:, :, lanes(slab)], out_hbm.at[:, :, lanes(slab)], result_s
        )

    def order_back(phase):
        def one(step, carry):
            source_chip = lax.rem(16 - slab_of(step) + 2 * chip, 8)
            def arrived(blocks):
                pltpu.make_async_remote_copy(
                    src_ref=returned.at[phase, blocks],
                    dst_ref=returned.at[phase, blocks],
                    send_sem=out_s.at[phase],
                    recv_sem=out_r.at[phase, source_chip],
                    device_id={"mem": sibling},
                    device_id_type=MESH,
                ).wait_recv()

            pl.when(source_chip != chip)(lambda: arrived(pl.ds(2 * source_chip, 2)))
            pl.when(source_chip == chip)(lambda: arrived(pl.ds(sibling, 1)))
            for c in range(CHUNKS):
                a = returned[phase, 2 * source_chip, c].astype(F32)
                b = returned[phase, 2 * source_chip + 1, c].astype(F32)
                flat[pl.ds(2 * c, 16, stride=16), :] = jnp.where(first, a, pltpu.roll(b, 64, 1))
                flat[pl.ds(2 * c + 1, 16, stride=16), :] = jnp.where(first, pltpu.roll(a, 64, 1), b)
            ordered[:, :, lanes(phase * 8 + source_chip)] = flat[...].reshape(16, 16, 128).astype(BF16)
            result_copy(phase * 8 + source_chip).start()
            return carry

        lax.fori_loop(0, 8, one, 0)

    with stage("adjacent"):
        pass_barrier(1, 4, adjacent_in)
        for phase in range(2):
            for side in range(2):
                code_copy(phase, side).start()
    with stage("in_wait0"):
        in_wait(0)
    with stage("observe0"):
        observe(0)
    for side in range(2):
        pl.when(jnp.logical_not(y_wraps(side)))(lambda side=side: y_start(0, side))
    def second_in_rest():
        for i in SENDS[EARLY:]:
            second_in(i, False)

    with stage("second_in_b"):
        pl.when(jnp.logical_not(edge))(second_in_rest)
    with stage("edge"):

        @pl.when(edge)
        def _():
            in_wait(1)
            observe(1)
            for side in range(2):
                pl.when(y_wraps(side))(lambda side=side: y_start(0, side))
            second_in_rest()
            for side in range(2):
                y_start(1, side)

    with stage("center0"):
        center_state(0)
    with stage("sum_row0"):
        codes_all().wait_recv()
        sum_row(0)
    with stage("in_wait1"):
        pl.when(jnp.logical_not(edge))(lambda: in_wait(1))
    with stage("observe1"):

        @pl.when(jnp.logical_not(edge))
        def _():
            observe(1)
            for side in range(2):
                y_start(1, side)

    with stage("x_wait0"):
        x_wait(0)
    with stage("transform0"):
        weights = transform(0)
    with stage("apply0"):
        apply(0, weights)
    send_out(0, SENDS)
    with stage("center1"):
        keep_own(0)
        center_state(1)
    with stage("sum_row1"):
        sum_row(1)
    with stage("x_wait1"):
        x_wait(1)
    with stage("transform1"):
        weights = transform(1)
    with stage("apply1"):
        apply(1, weights)
    send_out(1, SENDS)
    keep_own(1)
    with stage("sent"):
        for phase in range(2):
            in_all(phase).wait_send()
            y_all(phase, slice(0, MSG)).wait_send()
            x_all(phase).wait_send()
        codes_all().wait_send()
        for j in range(2):
            pl.when(obs_far(j))(lambda j=j: obs_copy(j).wait_send())
    with stage("back0"):
        order_back(0)
    with stage("back1"):
        order_back(1)

    with stage("drain"):
        for phase in range(2):
            others = update.at[phase, :, pl.ds(0, K - 16), :]
            pltpu.make_async_remote_copy(
                src_ref=others,
                dst_ref=others,
                send_sem=out_s.at[phase],
                recv_sem=out_r.at[phase, chip],
                device_id={"mem": sibling},
                device_id_type=MESH,
            ).wait_send()
        pltpu.make_async_copy(ordered, out_hbm, result_s).wait()


def per_device(background, observations, obs_coef, obs_rinv, obs_site, obs_count, neighbours):
    dma = pltpu.SemaphoreType.DMA
    small = (observations, obs_coef, obs_rinv, obs_site, obs_count, neighbours)
    return pl.pallas_call(
        kernel,
        out_shape=jax.ShapeDtypeStruct(background.shape, BF16),
        in_specs=[pl.BlockSpec(memory_space=pltpu.HBM)] * 7,
        out_specs=pl.BlockSpec(memory_space=pl.ANY),
        scratch_shapes=[
            pltpu.VMEM(background.shape, BF16),
            *(pltpu.VMEM(array.shape, array.dtype) for array in small),
            pltpu.VMEM((256, 128), F32),
            pltpu.VMEM((2 * NMEM, CHUNKS, 16, 128), BF16),
            pltpu.VMEM((2, CHUNKS, K, 128), BF16),
            pltpu.VMEM((2, 16, OBS), F32),
            pltpu.VMEM((2, 16, OBS), F32),
            pltpu.VMEM((2, 2, 16, 128), F32),
            pltpu.VMEM((2, CHUNKS * 128, OBS), BF16),
            pltpu.VMEM((2, MSG, 128), F32),
            pltpu.VMEM((2, MSG, 128), BF16),
            pltpu.VMEM((2, 2, MSG, 128), BF16),
            pltpu.VMEM((2, MSG, 128), F32),
            pltpu.VMEM((2, 2, MSG, 128), BF16),
            pltpu.VMEM((2, 2, MSG, 128), BF16),
            pltpu.VMEM((2, K, CHUNKS * 128), BF16),
            pltpu.VMEM((2, 8, CHUNKS * 128), F32),
            pltpu.VMEM((2, CHUNKS, K, 128), BF16),
            pltpu.VMEM((2, NMEM, CHUNKS, 16, 128), BF16),
            pltpu.VMEM(background.shape, BF16),
            pltpu.SemaphoreType.REGULAR, pltpu.SemaphoreType.REGULAR,
            dma((2,)), dma((6,)),
            dma((2,)), dma((2,)),
            dma((2,)), dma((2,)),
            dma, dma,
            dma((2,)), dma((2, len(PARTS))),
            dma((2,)), dma((2,)),
            dma((2,)), dma((2, 8)),
            dma,
        ],
        compiler_params=pltpu.CompilerParams(
            collective_id=0, has_side_effects=True, vmem_limit_bytes=62 << 20
        ),
        name="analysis",
    )(background, *small)


def solution(mesh):
    in_specs = (
        P("mem", None, "reg"),
        P("reg", "mem", None),
        P("reg", "mem", None),
        P("reg", "mem", None),
        P("reg", "mem", None),
        P("reg", "mem"),
        P("reg", "mem", None),
    )
    out_specs = P("mem", None, "reg")
    return jax.shard_map(
        per_device, mesh=mesh, in_specs=in_specs, out_specs=out_specs, check_vma=False
    )
```

time: 85.2 us -> 75.8 us (0.89)
  Pallas kernels: 78.5 us -> 73.3 us
  local copies, waits for them, and re-layouts: 6.25 us -> 2.3 us
    pallas_call x2 -> x1, Pallas kernels: 78.5 us -> 73.3 us  [per_device(): pl.pallas_call(kernel, out_shape=jax.ShapeDtypeStruct(background.shape, B...]
    unnamed x16 -> x1, local copies, waits for them, and re-layouts: 6.25 us -> 2.3 us
where the time goes in v2:
time: 75.8 us; the launch traced here: 75.6 us
  Pallas kernels  73.3 us (97%)
  local copies, waits for them, and re-layouts  2.3 us (3%)
    pallas_call x1, Pallas kernels, per_device(): pl.pallas_call(kernel, out_shape=jax.ShapeDtypeStruct(background.shape, B...  73.3 us
    unnamed x1, local copies, waits for them, and re-layouts  2.3 us

profile of v2, /device:TPU:1, one launch (start us, length us, event | category | flops | bytes accessed | tf_op | source)
XLA Modules:
  0.0 75.6 jit_solution(3948835093231880707)
XLA Ops:
  0.0 73.3 %analysis.1 = bf16[16,16,2048]{2,1,0:T(8,128)(2,1)} custom-call(bf16[16,16,2048]{2,1,0:T(8,128)(2,1)} %x_hbm.1, f32[1,2,384]{2,1,0:T(2,128)} %obs_hbm.1, f32[1,2,384]{2,1,0:T(2,128)} %coef_hbm.1, f32[1,2,384]{2,1,0:T(2,128)} %rinv_hbm.1, s32[1,2,384]{2,1,0:T(2,128)} %site_hbm.1, s32[1,2]{1,0:T(1,128)} %count_hbm.1, s32[1,2,5]{2,1,0:T(2,128)} %near_hbm.1), custom_call_target="tpu_custom_call" | custom-call | tf_op jit(solution)/shard_map/analysis/pallas_call | solution.py:574
  73.3 2.3 %copy.9 = bf16[16,16,2048]{2,1,0:T(8,128)(2,1)} copy(bf16[16,16,2048]{2,1,0:T(8,128)(2,1)} %analysis.1) | data formatting | bytes 2097152

commit v3 on v2

--- a/solution.py
+++ b/solution.py
@@ -16,9 +16,9 @@
 K = 256
 OBS = 384
 CHUNKS = 8
-PACK = 384
-MSG = 400
-PARTS = ((0, 128), (128, 256), (256, MSG))
+PACK = 256
+MSG = 272
+PARTS = ((0, 128), (128, MSG))
 CODE_ROW = 5
 SENDS = tuple((away, core) for away in (3, 2, 1, 4, -3, -2, -1) for core in range(2)) + ((0, 0),)
 EARLY = 6
@@ -52,25 +52,41 @@
     return block
 
 
-def drive_rows(low_half, high_half):
+def tail_rows(tail):
+    low_half, high_half = tail[0:1] + tail[2:3], tail[1:2] + tail[3:4]
     a, b = low_half.astype(BF16).astype(F32), high_half.astype(BF16).astype(F32)
-    return rows_of([a, b, low_half - a, high_half - b], MSG - PACK).astype(BF16)
+    return rows_of([a, b, low_half - a, high_half - b, tail[4:5]], MSG - PACK).astype(BF16)
+
+
+def square_indices(n):
+    return lax.broadcasted_iota(jnp.int32, (n, n), 0), lax.broadcasted_iota(jnp.int32, (n, n), 1)
 
 
 def newton_root(matrix):
-    n = matrix.shape[0]
-    diagonal = lax.broadcasted_iota(jnp.int32, (n, n), 0) == lax.broadcasted_iota(jnp.int32, (n, n), 1)
-    eye15 = jnp.where(diagonal, 1.5, 0.0).astype(F32)
-    middle = eye15 - 0.5 * matrix
-    inverse = split2(middle)
-    current = split2(dot3(split2(matrix), inverse))
+    row, column = square_indices(matrix.shape[0])
+    level = jnp.sum(jnp.where(row == column, matrix, 0.0), axis=0, keepdims=True)
+    level = jnp.sum(level, axis=1, keepdims=True) * (1.0 / matrix.shape[0])
+
+    def product(left, right):
+        inner = dot(left[2], right[2])
+        return left[0] * right[0], left[0] * right[1] + (right[0] * left[1] + inner)
+
+    def rounded(value, rest):
+        return value, rest, rest.astype(BF16)
+
+    def middle_of(value, rest):
+        return rounded(1.5 - 0.5 * value, -0.5 * rest)
+
+    current = rounded(level, jnp.where(row == column, matrix - level, matrix))
+    middle = middle_of(*current[:2])
+    inverse = middle
+    current = rounded(*product(current, inverse))
     for step in range(1, NS_ITERS):
-        middle = split2(eye15 - 0.5 * dot3(inverse, current))
+        middle = middle_of(*product(inverse, current))
         if step < NS_ITERS - 1:
-            current = split2(dot3(current, middle))
-        product = dot3(middle, inverse)
-        inverse = split2(product)
-    return product
+            current = rounded(*product(current, middle))
+        inverse = rounded(*product(middle, inverse))
+    return jnp.where(row == column, inverse[0] + inverse[1], inverse[1])
 
 
 def stage(name):
@@ -89,7 +105,11 @@
     chip = me // 2
     left, right = lax.rem(me + NMEM - 1, NMEM), lax.rem(me + 1, NMEM)
     below, above = lax.rem(reg + NREG - 1, NREG), lax.rem(reg + 1, NREG)
-    edge = jnp.logical_or(me == 0, me == NMEM - 1)
+    ends = (me == 0, me == NMEM - 1)
+    edge = jnp.logical_or(*ends)
+
+    def block_of(phase, owner):
+        return owner if phase == 0 else 2 * NMEM - 1 - owner
 
     core = lax.rem(me, 2)
     sibling = me + 1 - 2 * core
@@ -155,7 +175,7 @@
 
     def in_copy(phase, target):
         return pltpu.make_async_remote_copy(
-            src_ref=packed.at[phase * NMEM + target],
+            src_ref=packed.at[block_of(phase, target)],
             dst_ref=recv.at[phase, :, mine, :],
             send_sem=in_s.at[phase],
             recv_sem=in_r.at[phase],
@@ -179,18 +199,22 @@
 
     half = me // 8
 
+    def obs_target(j):
+        block = 2 * me + j
+        return jnp.where(half == 0, block, 2 * NMEM - 1 - block)
+
     def obs_copy(j):
         return pltpu.make_async_remote_copy(
             src_ref=obs_send.at[j],
             dst_ref=obs_recv.at[half],
             send_sem=obs_s.at[j],
             recv_sem=obs_r.at[half],
-            device_id={"mem": lax.rem(2 * me + j, NMEM)},
+            device_id={"mem": obs_target(j)},
             device_id_type=MESH,
         )
 
     def obs_far(j):
-        return lax.rem(2 * me + j, NMEM) != me
+        return obs_target(j) != me
 
     def first_in(step, carry):
         slab = slab_of(step)
@@ -256,7 +280,7 @@
         for i in SENDS[:EARLY]:
             second_in(i, False)
         recv[0, :, mine, :] = packed[me]
-        recv[1, :, mine, :] = packed[NMEM + me]
+        recv[1, :, mine, :] = packed[block_of(1, me)]
 
     def code_copy(phase, side):
         return pltpu.make_async_remote_copy(
@@ -280,14 +304,16 @@
 
     with stage("onehot"):
         for phase in range(2):
-            @pl.when(phase * 8 + chip != me)
-            def _(phase=phase):
+            source = block_of(phase, me) // 2
+
+            @pl.when(source != me)
+            def _(phase=phase, source=source):
                 pltpu.make_async_remote_copy(
                     src_ref=obs_send.at[0],
                     dst_ref=obs_recv.at[phase],
                     send_sem=obs_s.at[0],
                     recv_sem=obs_r.at[phase],
-                    device_id={"mem": phase * 8 + chip},
+                    device_id={"mem": source},
                     device_id_type=MESH,
                 ).wait_recv()
 
@@ -309,19 +335,21 @@
         b = (misfit - a).astype(BF16).astype(F32)
         parts = rows_of([a, b, misfit - a - b], 16).astype(BF16)
         drive = jnp.sum(dot_nt(parts, scaled), axis=0, keepdims=True)
-        for i, block in enumerate((gram[:128, :128], gram[:128, 128:], gram[128:, 128:])):
+        row, column = square_indices(128)
+        upper, lower = gram[:128, :128], gram[128:, 128:]
+        diagonal = jnp.sum(jnp.where(row == column, lower, 0.0), axis=0, keepdims=True)
+        for i, block in enumerate((jnp.where(row <= column, upper, lower), gram[:128, 128:])):
             own[phase, i * 128 : (i + 1) * 128, :] = block
             gmsg[phase, i * 128 : (i + 1) * 128, :] = block.astype(BF16)
-        own[phase, PACK:MSG, :] = rows_of([drive[:, :128], drive[:, 128:]], MSG - PACK)
-        gmsg[phase, PACK:MSG, :] = drive_rows(drive[:, :128], drive[:, 128:])
-
-    def y_wraps(side):
-        return me == (NMEM - 1 if side == 0 else 0)
+        zero = jnp.zeros((1, 128), F32)
+        tail = rows_of([drive[:, :128], drive[:, 128:], zero, zero, diagonal], MSG - PACK)
+        own[phase, PACK:MSG, :] = tail
+        gmsg[phase, PACK:MSG, :] = tail_rows(tail)
 
     def y_copy(phase, side, part):
         rows = slice(*PARTS[part])
         return pltpu.make_async_remote_copy(
-            src_ref=gmsg.at[jnp.where(y_wraps(side), 1 - phase, phase), rows],
+            src_ref=gmsg.at[phase, rows],
             dst_ref=yrecv.at[phase, side, rows],
             send_sem=y_s.at[phase],
             recv_sem=y_r.at[phase, part],
@@ -329,9 +357,21 @@
             device_id_type=MESH,
         )
 
-    def y_start(phase, side):
-        for part in range(len(PARTS)):
-            y_copy(phase, side, part).start()
+    def y_start(phase):
+        for side in range(2):
+
+            @pl.when(jnp.logical_not(ends[1 - side]))
+            def _(side=side):
+                for part in range(len(PARTS)):
+                    y_copy(phase, side, part).start()
+
+    def y_turn():
+        for side in range(2):
+
+            @pl.when(ends[side])
+            def _(side=side):
+                for phase in range(2):
+                    yrecv[phase, side] = gmsg[1 - phase]
 
     def x_copy(phase, side, part):
         rows = slice(*PARTS[part])
@@ -344,16 +384,22 @@
             device_id_type=MESH,
         )
 
-    def y_all(phase, rows, part=0):
-        both = yrecv.at[phase, :, rows]
-        return pltpu.make_async_remote_copy(
-            src_ref=both,
-            dst_ref=both,
-            send_sem=y_s.at[phase],
-            recv_sem=y_r.at[phase, part],
-            device_id={"mem": sibling},
-            device_id_type=MESH,
-        )
+    def y_wait(phase, rows, part, sent):
+        def wait(sides):
+            ref = yrecv.at[phase, sides, rows]
+            copy = pltpu.make_async_remote_copy(
+                src_ref=ref,
+                dst_ref=ref,
+                send_sem=y_s.at[phase],
+                recv_sem=y_r.at[phase, part],
+                device_id={"mem": sibling},
+                device_id_type=MESH,
+            )
+            copy.wait_send() if sent else copy.wait_recv()
+
+        pl.when(ends[0])(lambda: wait(slice(1, 2)))
+        pl.when(ends[1])(lambda: wait(slice(0, 1)))
+        pl.when(jnp.logical_not(edge))(lambda: wait(slice(0, 2)))
 
     def x_all(phase):
         return pltpu.make_async_remote_copy(
@@ -379,23 +425,21 @@
         def weighted(weights, first_code, rows):
             w = [weights[CODE_ROW + first_code + i : CODE_ROW + first_code + i + 1, :] for i in range(3)]
             return (
-                w[0] * yrecv[phase, 0, rows, :].astype(F32)
+                w[0] * yrecv[phase, phase, rows, :].astype(F32)
                 + w[1] * own[phase, rows, :]
-                + w[2] * yrecv[phase, 1, rows, :].astype(F32)
+                + w[2] * yrecv[phase, 1 - phase, rows, :].astype(F32)
             )
 
         for part in range(len(PARTS)):
             rows = slice(part * 128, (part + 1) * 128)
-            y_all(phase, slice(*PARTS[part]), part).wait_recv()
+            y_wait(phase, slice(*PARTS[part]), part, False)
             for side in range(2):
                 weights = code_recv[phase, 1 - side]
                 first_code = 0 if side == 0 else 6
                 xsend[phase, side, rows, :] = weighted(weights, first_code, rows).astype(BF16)
                 if part == len(PARTS) - 1:
                     tail = weighted(weights, first_code, slice(PACK, MSG))
-                    xsend[phase, side, PACK:MSG, :] = drive_rows(
-                        tail[0:1] + tail[2:3], tail[1:2] + tail[3:4]
-                    )
+                    xsend[phase, side, PACK:MSG, :] = tail_rows(tail)
                 x_copy(phase, side, part).start()
         center[phase] = weighted(obs_recv[phase, :, 0:128], 3, slice(0, MSG))
 
@@ -403,16 +447,18 @@
         total = center[phase] + xrecv[phase, 0].astype(F32) + xrecv[phase, 1].astype(F32)
         tail = total[PACK:MSG]
         drive = jnp.concatenate([tail[0:1] + tail[2:3], tail[1:2] + tail[3:4]], axis=1)
-        corner = total[128:256]
+        row, column = square_indices(128)
+        corner, cut = total[128:256], total[0:128]
+        turned = cut.T
+        first_block = jnp.where(row <= column, cut, turned) + jnp.where(row == column, K - 1.0, 0.0)
+        last_block = jnp.where(row == column, tail[4:5] + (K - 1.0), jnp.where(row > column, cut, turned))
         system = jnp.concatenate(
             [
-                jnp.concatenate([total[0:128], corner], axis=1),
-                jnp.concatenate([corner.T, total[256:384]], axis=1),
+                jnp.concatenate([first_block, corner], axis=1),
+                jnp.concatenate([corner.T, last_block], axis=1),
             ],
             axis=0,
         )
-        diagonal = lax.broadcasted_iota(jnp.int32, (K, K), 0) == lax.broadcasted_iota(jnp.int32, (K, K), 1)
-        system = system + jnp.where(diagonal, K - 1.0, 0.0)
         scale = jnp.max(jnp.sum(jnp.abs(system), axis=0, keepdims=True), axis=1, keepdims=True)
         half_root = newton_root(system / scale) / jnp.sqrt(scale)
         halves = split2(half_root)
@@ -467,12 +513,13 @@
             pl.when(source_chip != chip)(lambda: arrived(pl.ds(2 * source_chip, 2)))
             pl.when(source_chip == chip)(lambda: arrived(pl.ds(sibling, 1)))
             for c in range(CHUNKS):
-                a = returned[phase, 2 * source_chip, c].astype(F32)
-                b = returned[phase, 2 * source_chip + 1, c].astype(F32)
+                a = returned[phase, 2 * source_chip + phase, c].astype(F32)
+                b = returned[phase, 2 * source_chip + 1 - phase, c].astype(F32)
                 flat[pl.ds(2 * c, 16, stride=16), :] = jnp.where(first, a, pltpu.roll(b, 64, 1))
                 flat[pl.ds(2 * c + 1, 16, stride=16), :] = jnp.where(first, pltpu.roll(a, 64, 1), b)
-            ordered[:, :, lanes(phase * 8 + source_chip)] = flat[...].reshape(16, 16, 128).astype(BF16)
-            result_copy(phase * 8 + source_chip).start()
+            slab = source_chip if phase == 0 else 15 - source_chip
+            ordered[:, :, lanes(slab)] = flat[...].reshape(16, 16, 128).astype(BF16)
+            result_copy(slab).start()
             return carry
 
         lax.fori_loop(0, 8, one, 0)
@@ -486,8 +533,8 @@
         in_wait(0)
     with stage("observe0"):
         observe(0)
-    for side in range(2):
-        pl.when(jnp.logical_not(y_wraps(side)))(lambda side=side: y_start(0, side))
+    y_start(0)
+
     def second_in_rest():
         for i in SENDS[EARLY:]:
             second_in(i, False)
@@ -500,11 +547,9 @@
         def _():
             in_wait(1)
             observe(1)
-            for side in range(2):
-                pl.when(y_wraps(side))(lambda side=side: y_start(0, side))
+            y_turn()
+            y_start(1)
             second_in_rest()
-            for side in range(2):
-                y_start(1, side)
 
     with stage("center0"):
         center_state(0)
@@ -518,8 +563,7 @@
         @pl.when(jnp.logical_not(edge))
         def _():
             observe(1)
-            for side in range(2):
-                y_start(1, side)
+            y_start(1)
 
     with stage("x_wait0"):
         x_wait(0)
@@ -528,11 +572,11 @@
     with stage("apply0"):
         apply(0, weights)
     send_out(0, SENDS)
+    with stage("sum_row1"):
+        sum_row(1)
     with stage("center1"):
         keep_own(0)
         center_state(1)
-    with stage("sum_row1"):
-        sum_row(1)
     with stage("x_wait1"):
         x_wait(1)
     with stage("transform1"):
@@ -544,7 +588,7 @@
     with stage("sent"):
         for phase in range(2):
             in_all(phase).wait_send()
-            y_all(phase, slice(0, MSG)).wait_send()
+            y_wait(phase, slice(0, MSG), 0, True)
             x_all(phase).wait_send()
         codes_all().wait_send()
         for j in range(2):

time: 75.8 us -> 73.1 us (0.964)
  Pallas kernels: 73.3 us -> 70.6 us
    pallas_call x1, Pallas kernels: 73.3 us -> 70.6 us  [per_device(): pl.pallas_call(kernel, out_shape=jax.ShapeDtypeStruct(background.shape, B...]
where the time goes in v3:
time: 73.1 us; the launch traced here: 72.9 us
  Pallas kernels  70.6 us (97%)
  local copies, waits for them, and re-layouts  2.3 us (3%)
    pallas_call x1, Pallas kernels, per_device(): pl.pallas_call(kernel, out_shape=jax.ShapeDtypeStruct(background.shape, B...  70.6 us
    unnamed x1, local copies, waits for them, and re-layouts  2.3 us

profile of v3, /device:TPU:1, one launch (start us, length us, event | category | flops | bytes accessed | tf_op | source)
XLA Modules:
  0.0 72.9 jit_solution(8086209904290305127)
XLA Ops:
  0.0 70.6 %analysis.1 = bf16[16,16,2048]{2,1,0:T(8,128)(2,1)} custom-call(bf16[16,16,2048]{2,1,0:T(8,128)(2,1)} %x_hbm.1, f32[1,2,384]{2,1,0:T(2,128)} %obs_hbm.1, f32[1,2,384]{2,1,0:T(2,128)} %coef_hbm.1, f32[1,2,384]{2,1,0:T(2,128)} %rinv_hbm.1, s32[1,2,384]{2,1,0:T(2,128)} %site_hbm.1, s32[1,2]{1,0:T(1,128)} %count_hbm.1, s32[1,2,5]{2,1,0:T(2,128)} %near_hbm.1), custom_call_target="tpu_custom_call" | custom-call | tf_op jit(solution)/shard_map/analysis/pallas_call | solution.py:618
  70.6 2.3 %copy.9 = bf16[16,16,2048]{2,1,0:T(8,128)(2,1)} copy(bf16[16,16,2048]{2,1,0:T(8,128)(2,1)} %analysis.1) | data formatting | bytes 2097152

commit v4 on v3

--- a/solution.py
+++ b/solution.py
@@ -20,9 +20,8 @@
 MSG = 272
 PARTS = ((0, 128), (128, MSG))
 CODE_ROW = 5
-SENDS = tuple((away, core) for away in (3, 2, 1, 4, -3, -2, -1) for core in range(2)) + ((0, 0),)
+SENDS = tuple((away, core) for away in (4, 3, -3, 2, -2, 1, -1) for core in range(2)) + ((0, 0),)
 EARLY = 6
-EARLY_OUT = 6
 
 
 def split2(x):
@@ -96,9 +95,9 @@
 def kernel(
     x_hbm, obs_hbm, coef_hbm, rinv_hbm, site_hbm, count_hbm, near_hbm, out_hbm,
     state, obs_in, coef_in, rinv_in, site_in, count_in, near_in,
-    flat, packed, recv, obs_send, obs_recv, code_recv, onehot, own, gmsg, yrecv, center, xsend, xrecv,
+    flat, packed, recv, obs_send, obs_recv, code_recv, onehot, own, gmsg, ysend, yrecv, center, xsend, xrecv, turned,
     spread, mean, update, returned, ordered,
-    region_in, adjacent_in, state_s, small_s, in_s, in_r, obs_s, obs_r, code_s, code_r, y_s, y_r, x_s, x_r, out_s, out_r, result_s,
+    region_in, adjacent_in, state_s, small_s, in_s, in_r, obs_s, obs_r, code_s, code_r, y_s, y_r, x_s, x_r, turn_s, turn_r, out_s, out_r, result_s,
 ):
     me = lax.axis_index("mem")
     reg = lax.axis_index("reg")
@@ -119,7 +118,7 @@
         pl.semaphore_signal(barrier, inc=1, device_id={"mem": target}, device_id_type=MESH)
 
     pl.when(core == 1)(lambda: greet(sibling))
-    for i in range(1, 8):
+    for i in (4, 3, 5, 2, 6, 1, 7):
         greet(2 * lax.rem(chip + i, 8))
     for side in (below, above):
         pl.semaphore_signal(
@@ -227,9 +226,6 @@
     with stage("barrier"):
         state_copy(0).wait()
         pass_barrier(0, NMEM - 1, region_in)
-    with stage("first_in_a"):
-        lax.fori_loop(0, 2, first_in, 0)
-
     with stage("obs_send"):
         for copy in small:
             copy.wait()
@@ -268,8 +264,8 @@
         reorder(slab)
         return carry
 
-    with stage("first_in_b"):
-        lax.fori_loop(2, 8, first_in, 0)
+    with stage("first_in"):
+        lax.fori_loop(0, 8, first_in, 0)
     with stage("second_in"):
         state_copy(1).wait()
         reorder(8)
@@ -277,30 +273,50 @@
         for i in SENDS:
             second_in(i, True)
         lax.fori_loop(9, 15, reorder_step, 0)
-        for i in SENDS[:EARLY]:
-            second_in(i, False)
         recv[0, :, mine, :] = packed[me]
         recv[1, :, mine, :] = packed[block_of(1, me)]
 
     def code_copy(phase, side):
+        if phase == 0:
+            target = {"mem": right if side == 0 else left}
+        else:
+            target = {"reg": above if side == 0 else below}
         return pltpu.make_async_remote_copy(
             src_ref=obs_recv.at[phase, :, 0:128],
             dst_ref=code_recv.at[phase, side],
-            send_sem=code_s,
-            recv_sem=code_r,
-            device_id={"reg": above if side == 0 else below},
-            device_id_type=MESH,
-        )
-
-    def codes_all():
-        return pltpu.make_async_remote_copy(
-            src_ref=code_recv,
-            dst_ref=code_recv,
-            send_sem=code_s,
-            recv_sem=code_r,
-            device_id={"reg": above},
-            device_id_type=MESH,
-        )
+            send_sem=code_s.at[phase],
+            recv_sem=code_r.at[phase],
+            device_id=target,
+            device_id_type=MESH,
+        )
+
+    def along_line(copy):
+        for side in range(2):
+            pl.when(jnp.logical_not(ends[1 - side]))(lambda side=side: copy(side).start())
+
+    def sides_wait(ref, send_sem, recv_sem, sent):
+        copy = pltpu.make_async_remote_copy(
+            src_ref=ref,
+            dst_ref=ref,
+            send_sem=send_sem,
+            recv_sem=recv_sem,
+            device_id={"mem": sibling},
+            device_id_type=MESH,
+        )
+        copy.wait_send() if sent else copy.wait_recv()
+
+    def line_wait(ref_of, send_sem, recv_sem, sent):
+        pl.when(ends[0])(lambda: sides_wait(ref_of(slice(1, 2)), send_sem, recv_sem, sent))
+        pl.when(ends[1])(lambda: sides_wait(ref_of(slice(0, 1)), send_sem, recv_sem, sent))
+        pl.when(jnp.logical_not(edge))(
+            lambda: sides_wait(ref_of(slice(0, 2)), send_sem, recv_sem, sent)
+        )
+
+    def code_wait(phase, sent):
+        if phase == 0:
+            line_wait(lambda sides: code_recv.at[0, sides], code_s.at[0], code_r.at[0], sent)
+        else:
+            sides_wait(code_recv.at[1], code_s.at[1], code_r.at[1], sent)
 
     with stage("onehot"):
         for phase in range(2):
@@ -317,10 +333,20 @@
                     device_id_type=MESH,
                 ).wait_recv()
 
+            if phase == 0:
+                along_line(lambda side: code_copy(0, side))
             site = obs_recv[phase, 3:4, :].astype(jnp.int32)
             for c in range(CHUNKS):
                 place = lax.broadcasted_iota(jnp.int32, (128, OBS), 0) + c * 128
                 onehot[phase, c * 128 : (c + 1) * 128, :] = jnp.where(place == site, 1.0, 0.0).astype(BF16)
+
+    with stage("second_out"):
+        for i in SENDS[:EARLY]:
+            second_in(i, False)
+    with stage("adjacent"):
+        pass_barrier(1, 4, adjacent_in)
+        for side in range(2):
+            code_copy(1, side).start()
 
     def observe(phase):
         values = jnp.concatenate([recv[phase, c] for c in range(CHUNKS)], axis=1)
@@ -349,7 +375,7 @@
     def y_copy(phase, side, part):
         rows = slice(*PARTS[part])
         return pltpu.make_async_remote_copy(
-            src_ref=gmsg.at[phase, rows],
+            src_ref=ysend.at[side, rows] if phase == 0 else gmsg.at[1, rows],
             dst_ref=yrecv.at[phase, side, rows],
             send_sem=y_s.at[phase],
             recv_sem=y_r.at[phase, part],
@@ -357,26 +383,19 @@
             device_id_type=MESH,
         )
 
-    def y_start(phase):
-        for side in range(2):
-
-            @pl.when(jnp.logical_not(ends[1 - side]))
-            def _(side=side):
-                for part in range(len(PARTS)):
-                    y_copy(phase, side, part).start()
-
-    def y_turn():
-        for side in range(2):
-
-            @pl.when(ends[side])
-            def _(side=side):
-                for phase in range(2):
-                    yrecv[phase, side] = gmsg[1 - phase]
+    def y_wait(phase, rows, part, sent):
+        line_wait(
+            lambda sides: yrecv.at[phase, sides, rows], y_s.at[phase], y_r.at[phase, part], sent
+        )
+
+    def y_start():
+        for part in range(len(PARTS)):
+            along_line(lambda side, part=part: y_copy(1, side, part))
 
     def x_copy(phase, side, part):
         rows = slice(*PARTS[part])
         return pltpu.make_async_remote_copy(
-            src_ref=xsend.at[phase, side, rows],
+            src_ref=gmsg.at[0, rows] if phase == 0 else xsend.at[side, rows],
             dst_ref=xrecv.at[phase, side, rows],
             send_sem=x_s.at[phase],
             recv_sem=x_r.at[phase],
@@ -384,35 +403,18 @@
             device_id_type=MESH,
         )
 
-    def y_wait(phase, rows, part, sent):
-        def wait(sides):
-            ref = yrecv.at[phase, sides, rows]
-            copy = pltpu.make_async_remote_copy(
-                src_ref=ref,
-                dst_ref=ref,
-                send_sem=y_s.at[phase],
-                recv_sem=y_r.at[phase, part],
-                device_id={"mem": sibling},
-                device_id_type=MESH,
-            )
-            copy.wait_send() if sent else copy.wait_recv()
-
-        pl.when(ends[0])(lambda: wait(slice(1, 2)))
-        pl.when(ends[1])(lambda: wait(slice(0, 1)))
-        pl.when(jnp.logical_not(edge))(lambda: wait(slice(0, 2)))
-
-    def x_all(phase):
+    def x_wait(phase, sent=False):
+        sides_wait(xrecv.at[phase], x_s.at[phase], x_r.at[phase], sent)
+
+    def turn_copy(side):
         return pltpu.make_async_remote_copy(
-            src_ref=xsend.at[phase],
-            dst_ref=xrecv.at[phase],
-            send_sem=x_s.at[phase],
-            recv_sem=x_r.at[phase],
-            device_id={"reg": above},
-            device_id_type=MESH,
-        )
-
-    def x_wait(phase):
-        x_all(phase).wait_recv()
+            src_ref=gmsg.at[1],
+            dst_ref=turned.at[side],
+            send_sem=turn_s,
+            recv_sem=turn_r,
+            device_id={"reg": above if side == 0 else below},
+            device_id_type=MESH,
+        )
 
     def center_state(phase):
         for c in range(CHUNKS):
@@ -421,30 +423,62 @@
             mean[phase, :, c * 128 : (c + 1) * 128] = jnp.broadcast_to(average, (8, 128))
             spread[phase, :, c * 128 : (c + 1) * 128] = (values - average).astype(BF16)
 
-    def sum_row(phase):
-        def weighted(weights, first_code, rows):
-            w = [weights[CODE_ROW + first_code + i : CODE_ROW + first_code + i + 1, :] for i in range(3)]
-            return (
-                w[0] * yrecv[phase, phase, rows, :].astype(F32)
-                + w[1] * own[phase, rows, :]
-                + w[2] * yrecv[phase, 1 - phase, rows, :].astype(F32)
-            )
-
+    def weighted(weights, codes, terms, rows):
+        total = None
+        for code, term in zip(codes, terms):
+            term = weights[CODE_ROW + code : CODE_ROW + code + 1, :] * term[rows, :].astype(F32)
+            total = term if total is None else total + term
+        return total
+
+    def part_sum(target, weights, codes, terms, part):
+        rows = slice(part * 128, (part + 1) * 128)
+        target[rows, :] = weighted(weights, codes, terms, rows).astype(BF16)
+        if part == len(PARTS) - 1:
+            target[PACK:MSG, :] = tail_rows(weighted(weights, codes, terms, slice(PACK, MSG)))
+
+    def keep_turn(side):
+        yrecv[1, side] = gmsg[0]
+
+    def sum_column():
+        x_wait(0)
+        code_wait(0, False)
+        terms = (xrecv.at[0, 0], own.at[0], xrecv.at[0, 1])
         for part in range(len(PARTS)):
-            rows = slice(part * 128, (part + 1) * 128)
-            y_wait(phase, slice(*PARTS[part]), part, False)
             for side in range(2):
-                weights = code_recv[phase, 1 - side]
-                first_code = 0 if side == 0 else 6
-                xsend[phase, side, rows, :] = weighted(weights, first_code, rows).astype(BF16)
-                if part == len(PARTS) - 1:
-                    tail = weighted(weights, first_code, slice(PACK, MSG))
-                    xsend[phase, side, PACK:MSG, :] = tail_rows(tail)
-                x_copy(phase, side, part).start()
-        center[phase] = weighted(obs_recv[phase, :, 0:128], 3, slice(0, MSG))
+                codes = (0, 3, 6) if side == 0 else (2, 5, 8)
+
+                @pl.when(jnp.logical_not(ends[1 - side]))
+                def _(side=side, codes=codes):
+                    part_sum(ysend.at[side], code_recv[0, 1 - side], codes, terms, part)
+                    y_copy(0, side, part).start()
+
+        center[0] = weighted(obs_recv[0, :, 0:128], (1, 4, 7), terms, slice(0, MSG))
+
+    def sum_turn():
+        sides_wait(turned, turn_s, turn_r, False)
+        terms = (turned.at[0], own.at[1], turned.at[1])
+        for side in range(2):
+
+            @pl.when(ends[side])
+            def _(side=side):
+                for part in range(len(PARTS)):
+                    codes = (0, 3, 6) if side == 0 else (2, 5, 8)
+                    part_sum(yrecv.at[0, side], obs_recv[0, :, 0:128], codes, terms, part)
+
+    def sum_row():
+        code_wait(1, False)
+        terms = (yrecv.at[1, 1], own.at[1], yrecv.at[1, 0])
+        for part in range(len(PARTS)):
+            y_wait(1, slice(*PARTS[part]), part, False)
+            for side in range(2):
+                codes = (0, 1, 2) if side == 0 else (6, 7, 8)
+                part_sum(xsend.at[side], code_recv[1, 1 - side], codes, terms, part)
+                x_copy(1, side, part).start()
+        center[1] = weighted(obs_recv[1, :, 0:128], (3, 4, 5), terms, slice(0, MSG))
 
     def transform(phase):
-        total = center[phase] + xrecv[phase, 0].astype(F32) + xrecv[phase, 1].astype(F32)
+        sides = yrecv if phase == 0 else xrecv
+        total = center[phase] + sides[phase, 0].astype(F32) + sides[phase, 1].astype(F32)
         tail = total[PACK:MSG]
         drive = jnp.concatenate([tail[0:1] + tail[2:3], tail[1:2] + tail[3:4]], axis=1)
         row, column = square_indices(128)
@@ -524,38 +558,30 @@
 
         lax.fori_loop(0, 8, one, 0)
 
-    with stage("adjacent"):
-        pass_barrier(1, 4, adjacent_in)
-        for phase in range(2):
-            for side in range(2):
-                code_copy(phase, side).start()
     with stage("in_wait0"):
         in_wait(0)
     with stage("observe0"):
         observe(0)
-    y_start(0)
-
-    def second_in_rest():
+        for part in range(len(PARTS)):
+            for side in range(2):
+                x_copy(0, side, part).start()
         for i in SENDS[EARLY:]:
             second_in(i, False)
-
-    with stage("second_in_b"):
-        pl.when(jnp.logical_not(edge))(second_in_rest)
     with stage("edge"):
 
         @pl.when(edge)
         def _():
             in_wait(1)
             observe(1)
-            y_turn()
-            y_start(1)
-            second_in_rest()
+            for side in range(2):
+                turn_copy(side).start()
+                pl.when(ends[side])(lambda side=side: keep_turn(side))
+            y_start()
 
     with stage("center0"):
         center_state(0)
-    with stage("sum_row0"):
-        codes_all().wait_recv()
-        sum_row(0)
+    with stage("sum_column"):
+        sum_column()
     with stage("in_wait1"):
         pl.when(jnp.logical_not(edge))(lambda: in_wait(1))
     with stage("observe1"):
@@ -563,17 +589,20 @@
         @pl.when(jnp.logical_not(edge))
         def _():
             observe(1)
-            y_start(1)
-
-    with stage("x_wait0"):
-        x_wait(0)
+            y_start()
+
+    with stage("sum_turn"):
+        pl.when(edge)(sum_turn)
+    with stage("y_wait0"):
+        for part in range(len(PARTS)):
+            y_wait(0, slice(*PARTS[part]), part, False)
     with stage("transform0"):
         weights = transform(0)
     with stage("apply0"):
         apply(0, weights)
     send_out(0, SENDS)
     with stage("sum_row1"):
-        sum_row(1)
+        sum_row()
     with stage("center1"):
         keep_own(0)
         center_state(1)
@@ -589,8 +618,9 @@
         for phase in range(2):
             in_all(phase).wait_send()
             y_wait(phase, slice(0, MSG), 0, True)
-            x_all(phase).wait_send()
-        codes_all().wait_send()
+            x_wait(phase, True)
+            code_wait(phase, True)
+        pl.when(edge)(lambda: sides_wait(turned, turn_s, turn_r, True))
         for j in range(2):
             pl.when(obs_far(j))(lambda j=j: obs_copy(j).wait_send())
     with stage("back0"):
@@ -632,10 +662,12 @@
             pltpu.VMEM((2, CHUNKS * 128, OBS), BF16),
             pltpu.VMEM((2, MSG, 128), F32),
             pltpu.VMEM((2, MSG, 128), BF16),
+            pltpu.VMEM((2, MSG, 128), BF16),
             pltpu.VMEM((2, 2, MSG, 128), BF16),
             pltpu.VMEM((2, MSG, 128), F32),
+            pltpu.VMEM((2, MSG, 128), BF16),
             pltpu.VMEM((2, 2, MSG, 128), BF16),
-            pltpu.VMEM((2, 2, MSG, 128), BF16),
+            pltpu.VMEM((2, MSG, 128), BF16),
             pltpu.VMEM((2, K, CHUNKS * 128), BF16),
             pltpu.VMEM((2, 8, CHUNKS * 128), F32),
             pltpu.VMEM((2, CHUNKS, K, 128), BF16),
@@ -645,9 +677,10 @@
             dma((2,)), dma((6,)),
             dma((2,)), dma((2,)),
             dma((2,)), dma((2,)),
-            dma, dma,
+            dma((2,)), dma((2,)),
             dma((2,)), dma((2, len(PARTS))),
             dma((2,)), dma((2,)),
+            dma, dma,
             dma((2,)), dma((2, 8)),
             dma,
         ],

time: 73.1 us -> 70.5 us (0.964)
  Pallas kernels: 70.6 us -> 68 us
    pallas_call x1, Pallas kernels: 70.6 us -> 68 us  [per_device(): pl.pallas_call(kernel, out_shape=jax.ShapeDtypeStruct(background.shape, B...]
where the time goes in v4:
time: 70.5 us; the launch traced here: 70.4 us
  Pallas kernels  68 us (96%)
  local copies, waits for them, and re-layouts  2.3 us (3%)
    pallas_call x1, Pallas kernels, per_device(): pl.pallas_call(kernel, out_shape=jax.ShapeDtypeStruct(background.shape, B...  68 us
    unnamed x1, local copies, waits for them, and re-layouts  2.3 us

profile of v4, /device:TPU:1, one launch (start us, length us, event | category | flops | bytes accessed | tf_op | source)
XLA Modules:
  0.0 70.4 jit_solution(8126810379396714798)
XLA Ops:
  0.0 68.0 %analysis.1 = bf16[16,16,2048]{2,1,0:T(8,128)(2,1)} custom-call(bf16[16,16,2048]{2,1,0:T(8,128)(2,1)} %x_hbm.1, f32[1,2,384]{2,1,0:T(2,128)} %obs_hbm.1, f32[1,2,384]{2,1,0:T(2,128)} %coef_hbm.1, f32[1,2,384]{2,1,0:T(2,128)} %rinv_hbm.1, s32[1,2,384]{2,1,0:T(2,128)} %site_hbm.1, s32[1,2]{1,0:T(1,128)} %count_hbm.1, s32[1,2,5]{2,1,0:T(2,128)} %near_hbm.1), custom_call_target="tpu_custom_call" | custom-call | tf_op jit(solution)/shard_map/analysis/pallas_call | solution.py:648
  68.0 2.3 %copy.9 = bf16[16,16,2048]{2,1,0:T(8,128)(2,1)} copy(bf16[16,16,2048]{2,1,0:T(8,128)(2,1)} %analysis.1) | data formatting | bytes 2097152

commit v5 on v4

--- a/solution.py
+++ b/solution.py
@@ -95,7 +95,7 @@
 def kernel(
     x_hbm, obs_hbm, coef_hbm, rinv_hbm, site_hbm, count_hbm, near_hbm, out_hbm,
     state, obs_in, coef_in, rinv_in, site_in, count_in, near_in,
-    flat, packed, recv, obs_send, obs_recv, code_recv, onehot, own, gmsg, ysend, yrecv, center, xsend, xrecv, turned,
+    flat, packed, recv, obs_send, obs_recv, codes, code_recv, onehot, own, gmsg, ysend, yrecv, center, xsend, xrecv, turned,
     spread, mean, update, returned, ordered,
     region_in, adjacent_in, state_s, small_s, in_s, in_r, obs_s, obs_r, code_s, code_r, y_s, y_r, x_s, x_r, turn_s, turn_r, out_s, out_r, result_s,
 ):
@@ -229,15 +229,15 @@
     with stage("obs_send"):
         for copy in small:
             copy.wait()
-        row = lax.broadcasted_iota(jnp.int32, (16, OBS), 0)
-        code = row - CODE_ROW
-        away = jnp.abs(code // 3 - 1) + jnp.abs(lax.rem(code + 15, 3) - 1)
+        row = lax.broadcasted_iota(jnp.int32, (8, OBS), 0)
+        code = lax.broadcasted_iota(jnp.int32, (8, OBS), 1)
+        away = jnp.abs(code // 3 - 1) + jnp.abs(lax.rem(code, 3) - 1)
         taper = jnp.where(away == 0, 1.0, jnp.where(away == 1, 0.5, 0.25))
         for j in range(2):
             block = jnp.where(code == 4, 1.0, 0.0)
             for i in range(5):
                 block = block + jnp.where(code == near_in[0, j : j + 1, i : i + 1], taper, 0.0)
-            count = jnp.broadcast_to(count_in[0:1, j : j + 1].astype(F32), (16, OBS))
+            count = jnp.broadcast_to(count_in[0:1, j : j + 1].astype(F32), (8, OBS))
             obs_send[j] = jnp.where(row == 4, count, block)
             for i, ref in enumerate((obs_in, coef_in, rinv_in)):
                 obs_send[j, i : i + 1, :] = ref[0, j : j + 1, :]
@@ -282,7 +282,7 @@
         else:
             target = {"reg": above if side == 0 else below}
         return pltpu.make_async_remote_copy(
-            src_ref=obs_recv.at[phase, :, 0:128],
+            src_ref=codes.at[phase],
             dst_ref=code_recv.at[phase, side],
             send_sem=code_s.at[phase],
             recv_sem=code_r.at[phase],
@@ -333,6 +333,9 @@
                     device_id_type=MESH,
                 ).wait_recv()
 
+            row, column = (lax.broadcasted_iota(jnp.int32, (16, 128), axis) for axis in range(2))
+            weights = jnp.where(row - CODE_ROW == column, obs_recv[phase, 5:6, 0:128], 0.0)
+            codes[phase] = jnp.broadcast_to(jnp.sum(weights, axis=1, keepdims=True), (16, 128))
             if phase == 0:
                 along_line(lambda side: code_copy(0, side))
             site = obs_recv[phase, 3:4, :].astype(jnp.int32)
@@ -398,13 +401,13 @@
             src_ref=gmsg.at[0, rows] if phase == 0 else xsend.at[side, rows],
             dst_ref=xrecv.at[phase, side, rows],
             send_sem=x_s.at[phase],
-            recv_sem=x_r.at[phase],
+            recv_sem=x_r.at[phase, part],
             device_id={"reg": above if side == 0 else below},
             device_id_type=MESH,
         )
 
-    def x_wait(phase, sent=False):
-        sides_wait(xrecv.at[phase], x_s.at[phase], x_r.at[phase], sent)
+    def x_wait(phase, rows, part, sent):
+        sides_wait(xrecv.at[phase, :, rows], x_s.at[phase], x_r.at[phase, part], sent)
 
     def turn_copy(side):
         return pltpu.make_async_remote_copy(
@@ -423,36 +426,36 @@
             mean[phase, :, c * 128 : (c + 1) * 128] = jnp.broadcast_to(average, (8, 128))
             spread[phase, :, c * 128 : (c + 1) * 128] = (values - average).astype(BF16)
 
-    def weighted(weights, codes, terms, rows):
+    def weighted(weights, seen, terms, rows):
         total = None
-        for code, term in zip(codes, terms):
+        for code, term in zip(seen, terms):
             term = weights[CODE_ROW + code : CODE_ROW + code + 1, :] * term[rows, :].astype(F32)
             total = term if total is None else total + term
         return total
 
-    def part_sum(target, weights, codes, terms, part):
+    def part_sum(target, weights, seen, terms, part):
         rows = slice(part * 128, (part + 1) * 128)
-        target[rows, :] = weighted(weights, codes, terms, rows).astype(BF16)
+        target[rows, :] = weighted(weights, seen, terms, rows).astype(BF16)
         if part == len(PARTS) - 1:
-            target[PACK:MSG, :] = tail_rows(weighted(weights, codes, terms, slice(PACK, MSG)))
+            target[PACK:MSG, :] = tail_rows(weighted(weights, seen, terms, slice(PACK, MSG)))
 
     def keep_turn(side):
         yrecv[1, side] = gmsg[0]
 
     def sum_column():
-        x_wait(0)
         code_wait(0, False)
         terms = (xrecv.at[0, 0], own.at[0], xrecv.at[0, 1])
         for part in range(len(PARTS)):
+            x_wait(0, slice(*PARTS[part]), part, False)
             for side in range(2):
-                codes = (0, 3, 6) if side == 0 else (2, 5, 8)
+                seen = (0, 3, 6) if side == 0 else (2, 5, 8)
 
                 @pl.when(jnp.logical_not(ends[1 - side]))
-                def _(side=side, codes=codes):
-                    part_sum(ysend.at[side], code_recv[0, 1 - side], codes, terms, part)
+                def _(side=side, seen=seen):
+                    part_sum(ysend.at[side], code_recv[0, 1 - side], seen, terms, part)
                     y_copy(0, side, part).start()
 
-        center[0] = weighted(obs_recv[0, :, 0:128], (1, 4, 7), terms, slice(0, MSG))
+        center[0] = weighted(codes[0], (1, 4, 7), terms, slice(0, MSG))
 
     def sum_turn():
         sides_wait(turned, turn_s, turn_r, False)
@@ -462,8 +465,8 @@
             @pl.when(ends[side])
             def _(side=side):
                 for part in range(len(PARTS)):
-                    codes = (0, 3, 6) if side == 0 else (2, 5, 8)
-                    part_sum(yrecv.at[0, side], obs_recv[0, :, 0:128], codes, terms, part)
+                    seen = (0, 3, 6) if side == 0 else (2, 5, 8)
+                    part_sum(yrecv.at[0, side], codes[0], seen, terms, part)
 
     def sum_row():
         code_wait(1, False)
@@ -471,10 +474,10 @@
         for part in range(len(PARTS)):
             y_wait(1, slice(*PARTS[part]), part, False)
             for side in range(2):
-                codes = (0, 1, 2) if side == 0 else (6, 7, 8)
-                part_sum(xsend.at[side], code_recv[1, 1 - side], codes, terms, part)
+                seen = (0, 1, 2) if side == 0 else (6, 7, 8)
+                part_sum(xsend.at[side], code_recv[1, 1 - side], seen, terms, part)
                 x_copy(1, side, part).start()
-        center[1] = weighted(obs_recv[1, :, 0:128], (3, 4, 5), terms, slice(0, MSG))
+        center[1] = weighted(codes[1], (3, 4, 5), terms, slice(0, MSG))
 
     def transform(phase):
         sides = yrecv if phase == 0 else xrecv
@@ -607,7 +610,8 @@
         keep_own(0)
         center_state(1)
     with stage("x_wait1"):
-        x_wait(1)
+        for part in range(len(PARTS)):
+            x_wait(1, slice(*PARTS[part]), part, False)
     with stage("transform1"):
         weights = transform(1)
     with stage("apply1"):
@@ -618,7 +622,7 @@
         for phase in range(2):
             in_all(phase).wait_send()
             y_wait(phase, slice(0, MSG), 0, True)
-            x_wait(phase, True)
+            x_wait(phase, slice(0, MSG), 0, True)
             code_wait(phase, True)
         pl.when(edge)(lambda: sides_wait(turned, turn_s, turn_r, True))
         for j in range(2):
@@ -642,10 +646,14 @@
         pltpu.make_async_copy(ordered, out_hbm, result_s).wait()
 
 
+def hand_over(in_ref, out_ref):
+    out_ref[...] = in_ref[...]
+
+
 def per_device(background, observations, obs_coef, obs_rinv, obs_site, obs_count, neighbours):
     dma = pltpu.SemaphoreType.DMA
     small = (observations, obs_coef, obs_rinv, obs_site, obs_count, neighbours)
-    return pl.pallas_call(
+    ordered = pl.pallas_call(
         kernel,
         out_shape=jax.ShapeDtypeStruct(background.shape, BF16),
         in_specs=[pl.BlockSpec(memory_space=pltpu.HBM)] * 7,
@@ -656,8 +664,9 @@
             pltpu.VMEM((256, 128), F32),
             pltpu.VMEM((2 * NMEM, CHUNKS, 16, 128), BF16),
             pltpu.VMEM((2, CHUNKS, K, 128), BF16),
-            pltpu.VMEM((2, 16, OBS), F32),
-            pltpu.VMEM((2, 16, OBS), F32),
+            pltpu.VMEM((2, 8, OBS), F32),
+            pltpu.VMEM((2, 8, OBS), F32),
+            pltpu.VMEM((2, 16, 128), F32),
             pltpu.VMEM((2, 2, 16, 128), F32),
             pltpu.VMEM((2, CHUNKS * 128, OBS), BF16),
             pltpu.VMEM((2, MSG, 128), F32),
@@ -679,7 +688,7 @@
             dma((2,)), dma((2,)),
             dma((2,)), dma((2,)),
             dma((2,)), dma((2, len(PARTS))),
-            dma((2,)), dma((2,)),
+            dma((2,)), dma((2, len(PARTS))),
             dma, dma,
             dma((2,)), dma((2, 8)),
             dma,
@@ -689,6 +698,16 @@
         ),
         name="analysis",
     )(background, *small)
+    half = pl.BlockSpec((8, 16, background.shape[2]), lambda i: (i, 0, 0))
+    return pl.pallas_call(
+        hand_over,
+        grid=(2,),
+        out_shape=jax.ShapeDtypeStruct(background.shape, BF16),
+        in_specs=[half],
+        out_specs=half,
+        compiler_params=pltpu.CompilerParams(vmem_limit_bytes=60 << 20),
+        name="hand_over",
+    )(ordered)
 
 
 def solution(mesh):

time: 70.5 us -> 69.4 us (0.984)
  local copies, waits for them, and re-layouts: 2.3 us -> 0 us
  Pallas kernels: 68 us -> 69.2 us
    unnamed x1 -> x0, local copies, waits for them, and re-layouts: 2.3 us -> none
    pallas_call x0 -> x1, Pallas kernels: none -> 2.05 us  [per_device(): pl.pallas_call(hand_over, grid=(2,), out_shape=jax.ShapeDtypeStruct(backg...]
    pallas_call x1, Pallas kernels: 68 us -> 67.2 us  [per_device(): pl.pallas_call(kernel, out_shape=jax.ShapeDtypeStruct(background.shape, B...]
where the time goes in v5:
time: 69.4 us; the launch traced here: 69.2 us
  Pallas kernels  69.2 us (100%)
    pallas_call x1, Pallas kernels, per_device(): pl.pallas_call(kernel, out_shape=jax.ShapeDtypeStruct(background.shape, B...  67.2 us
    pallas_call x1, Pallas kernels, per_device(): pl.pallas_call(hand_over, grid=(2,), out_shape=jax.ShapeDtypeStruct(backg...  2.05 us

profile of v5, /device:TPU:1, one launch (start us, length us, event | category | flops | bytes accessed | tf_op | source)
XLA Modules:
  0.0 69.2 jit_solution(16154360342622359217)
XLA Ops:
  0.0 67.2 %analysis.1.in_ref = bf16[16,16,2048]{2,1,0:T(8,128)(2,1)} custom-call(bf16[16,16,2048]{2,1,0:T(8,128)(2,1)} %x_hbm.1, f32[1,2,384]{2,1,0:T(2,128)} %obs_hbm.1, f32[1,2,384]{2,1,0:T(2,128)} %coef_hbm.1, f32[1,2,384]{2,1,0:T(2,128)} %rinv_hbm.1, s32[1,2,384]{2,1,0:T(2,128)} %site_hbm.1, s32[1,2]{1,0:T(1,128)} %count_hbm.1, s32[1,2,5]{2,1,0:T(2,128)} %near_hbm.1), custom_call_target="tpu_custom_call" | custom-call | tf_op jit(solution)/shard_map/analysis/pallas_call | solution.py:656
  67.2 2.1 %hand_over.1 = bf16[16,16,2048]{2,1,0:T(8,128)(2,1)} custom-call(bf16[16,16,2048]{2,1,0:T(8,128)(2,1)} %analysis.1.in_ref), custom_call_target="tpu_custom_call" | custom-call | tf_op jit(solution)/shard_map/hand_over/pallas_call | solution.py:702

commit v6 on v5

--- a/solution.py
+++ b/solution.py
@@ -24,22 +24,12 @@
 EARLY = 6
 
 
-def split2(x):
-    high = x.astype(BF16)
-    low = (x - high.astype(F32)).astype(BF16)
-    return high, low
-
-
 def dot(a, b):
     return jnp.dot(a, b, preferred_element_type=F32)
 
 
 def dot_nt(a, b):
     return lax.dot_general(a, b, (((1,), (1,)), ((), ())), preferred_element_type=F32)
-
-
-def dot3(a, b):
-    return dot(a[0], b[0]) + (dot(a[0], b[1]) + dot(a[1], b[0]))
 
 
 def rows_of(parts, rows):
@@ -85,7 +75,7 @@
         if step < NS_ITERS - 1:
             current = rounded(*product(current, middle))
         inverse = rounded(*product(middle, inverse))
-    return jnp.where(row == column, inverse[0] + inverse[1], inverse[1])
+    return inverse
 
 
 def stage(name):
@@ -351,7 +341,7 @@
         for side in range(2):
             code_copy(1, side).start()
 
-    def observe(phase):
+    def observe(phase, part_done):
         values = jnp.concatenate([recv[phase, c] for c in range(CHUNKS)], axis=1)
         predicted = dot(values, onehot[phase]) * obs_recv[phase, 1:2, :]
         mean_pred = jnp.sum(predicted, axis=0, keepdims=True) * (1.0 / K)
@@ -360,20 +350,24 @@
         scaled = (root * (predicted - mean_pred)).astype(BF16)
         misfit = root * (obs_recv[phase, 0:1, :] - mean_pred)
         gram = dot_nt(scaled, scaled)
+        row, column = square_indices(128)
+        upper, lower = gram[:128, :128], gram[128:, 128:]
+        cut = jnp.where(row <= column, upper, lower)
+        own[phase, 0:128, :] = cut
+        gmsg[phase, 0:128, :] = cut.astype(BF16)
+        part_done(0)
+        diagonal = jnp.sum(jnp.where(row == column, lower, 0.0), axis=0, keepdims=True)
         a = misfit.astype(BF16).astype(F32)
         b = (misfit - a).astype(BF16).astype(F32)
         parts = rows_of([a, b, misfit - a - b], 16).astype(BF16)
         drive = jnp.sum(dot_nt(parts, scaled), axis=0, keepdims=True)
-        row, column = square_indices(128)
-        upper, lower = gram[:128, :128], gram[128:, 128:]
-        diagonal = jnp.sum(jnp.where(row == column, lower, 0.0), axis=0, keepdims=True)
-        for i, block in enumerate((jnp.where(row <= column, upper, lower), gram[:128, 128:])):
-            own[phase, i * 128 : (i + 1) * 128, :] = block
-            gmsg[phase, i * 128 : (i + 1) * 128, :] = block.astype(BF16)
+        own[phase, 128:256, :] = gram[:128, 128:]
+        gmsg[phase, 128:256, :] = gram[:128, 128:].astype(BF16)
         zero = jnp.zeros((1, 128), F32)
         tail = rows_of([drive[:, :128], drive[:, 128:], zero, zero, diagonal], MSG - PACK)
         own[phase, PACK:MSG, :] = tail
         gmsg[phase, PACK:MSG, :] = tail_rows(tail)
+        part_done(1)
 
     def y_copy(phase, side, part):
         rows = slice(*PARTS[part])
@@ -391,9 +385,12 @@
             lambda sides: yrecv.at[phase, sides, rows], y_s.at[phase], y_r.at[phase, part], sent
         )
 
-    def y_start():
-        for part in range(len(PARTS)):
-            along_line(lambda side, part=part: y_copy(1, side, part))
+    def y_start(part):
+        along_line(lambda side: y_copy(1, side, part))
+
+    def x_start(part):
+        for side in range(2):
+            x_copy(0, side, part).start()
 
     def x_copy(phase, side, part):
         rows = slice(*PARTS[part])
@@ -497,12 +494,17 @@
             axis=0,
         )
         scale = jnp.max(jnp.sum(jnp.abs(system), axis=0, keepdims=True), axis=1, keepdims=True)
-        half_root = newton_root(system / scale) / jnp.sqrt(scale)
-        halves = split2(half_root)
-        vector = jnp.broadcast_to(drive, (16, K))
-        vector = dot3(split2(vector), halves)
-        vector = dot3(split2(vector), halves)[0:1]
-        return (jnp.float32(K - 1.0) ** 0.5 * half_root + vector).astype(BF16)
+        level, rest, rounded_rest = newton_root(system * (1.0 / scale))
+        row, column = square_indices(K)
+        root = jnp.where(row == column, level + rest, rest)
+        high_row = lax.broadcasted_iota(jnp.int32, (16, K), 0) == 0
+        low_row = lax.broadcasted_iota(jnp.int32, (16, K), 0) == 1
+        vector = drive * (1.0 / scale)
+        for _ in range(2):
+            high = vector.astype(BF16).astype(F32)
+            parts = jnp.where(high_row, high, jnp.where(low_row, vector - high, 0.0)).astype(BF16)
+            vector = level * vector + jnp.sum(dot(parts, rounded_rest), axis=0, keepdims=True)
+        return (root * (jnp.float32(K - 1.0) ** 0.5 / jnp.sqrt(scale)) + vector).astype(BF16)
 
     def apply(phase, weights):
         for c in range(0, CHUNKS, 2):
@@ -564,10 +566,7 @@
     with stage("in_wait0"):
         in_wait(0)
     with stage("observe0"):
-        observe(0)
-        for part in range(len(PARTS)):
-            for side in range(2):
-                x_copy(0, side, part).start()
+        observe(0, x_start)
         for i in SENDS[EARLY:]:
             second_in(i, False)
     with stage("edge"):
@@ -575,11 +574,10 @@
         @pl.when(edge)
         def _():
             in_wait(1)
-            observe(1)
+            observe(1, y_start)
             for side in range(2):
                 turn_copy(side).start()
                 pl.when(ends[side])(lambda side=side: keep_turn(side))
-            y_start()
 
     with stage("center0"):
         center_state(0)
@@ -591,8 +589,7 @@
 
         @pl.when(jnp.logical_not(edge))
         def _():
-            observe(1)
-            y_start()
+            observe(1, y_start)
 
     with stage("sum_turn"):
         pl.when(edge)(sum_turn)

time: 69.4 us -> 69.2 us (level)
  no operation moved by 1% of the time
where the time goes in v6:
time: 69.2 us; the launch traced here: 69.1 us
  Pallas kernels  69.1 us (100%)
    pallas_call x1, Pallas kernels, per_device(): pl.pallas_call(kernel, out_shape=jax.ShapeDtypeStruct(background.shape, B...  67 us
    pallas_call x1, Pallas kernels, per_device(): pl.pallas_call(hand_over, grid=(2,), out_shape=jax.ShapeDtypeStruct(backg...  2.05 us

profile of v6, /device:TPU:1, one launch (start us, length us, event | category | flops | bytes accessed | tf_op | source)
XLA Modules:
  0.0 69.1 jit_solution(1076683903957693737)
XLA Ops:
  0.0 67.0 %analysis.1.in_ref = bf16[16,16,2048]{2,1,0:T(8,128)(2,1)} custom-call(bf16[16,16,2048]{2,1,0:T(8,128)(2,1)} %x_hbm.1, f32[1,2,384]{2,1,0:T(2,128)} %obs_hbm.1, f32[1,2,384]{2,1,0:T(2,128)} %coef_hbm.1, f32[1,2,384]{2,1,0:T(2,128)} %rinv_hbm.1, s32[1,2,384]{2,1,0:T(2,128)} %site_hbm.1, s32[1,2]{1,0:T(1,128)} %count_hbm.1, s32[1,2,5]{2,1,0:T(2,128)} %near_hbm.1), custom_call_target="tpu_custom_call" | custom-call | tf_op jit(solution)/shard_map/analysis/pallas_call | solution.py:653
  67.0 2.1 %hand_over.1 = bf16[16,16,2048]{2,1,0:T(8,128)(2,1)} custom-call(bf16[16,16,2048]{2,1,0:T(8,128)(2,1)} %analysis.1.in_ref), custom_call_target="tpu_custom_call" | custom-call | tf_op jit(solution)/shard_map/hand_over/pallas_call | solution.py:699

commit v7 on v6

--- a/solution.py
+++ b/solution.py
@@ -124,7 +124,7 @@
         pl.when(core != hearer)(lambda: pl.semaphore_wait(passed, 1))
 
     def slab_of(step):
-        away = 4 + lax.div(step + 1, 2) * (1 - 2 * lax.rem(step, 2))
+        away = 4 + lax.div(step + 1, 2) * (1 - 2 * lax.rem(step, 2)) * (1 - 2 * lax.rem(me, 2))
         return lax.rem(chip + away, 8)
 
     def lanes(slab):
@@ -519,7 +519,7 @@
             src_ref=update.at[phase, :, rows, :],
             dst_ref=returned.at[phase, me],
             send_sem=out_s.at[phase],
-            recv_sem=out_r.at[phase, chip],
+            recv_sem=out_r.at[8 if phase == 0 else chip],
             device_id={"mem": target},
             device_id_type=MESH,
         )
@@ -537,20 +537,18 @@
         )
 
     def order_back(phase):
+        def arrived(blocks, index):
+            blocks = returned.at[phase, blocks]
+            sides_wait(blocks, out_s.at[phase], out_r.at[index], False)
+
+        if phase == 0:
+            arrived(slice(0, NMEM - 1), 8)
+
         def one(step, carry):
             source_chip = lax.rem(16 - slab_of(step) + 2 * chip, 8)
-            def arrived(blocks):
-                pltpu.make_async_remote_copy(
-                    src_ref=returned.at[phase, blocks],
-                    dst_ref=returned.at[phase, blocks],
-                    send_sem=out_s.at[phase],
-                    recv_sem=out_r.at[phase, source_chip],
-                    device_id={"mem": sibling},
-                    device_id_type=MESH,
-                ).wait_recv()
-
-            pl.when(source_chip != chip)(lambda: arrived(pl.ds(2 * source_chip, 2)))
-            pl.when(source_chip == chip)(lambda: arrived(pl.ds(sibling, 1)))
+            if phase == 1:
+                pl.when(source_chip != chip)(lambda: arrived(pl.ds(2 * source_chip, 2), source_chip))
+                pl.when(source_chip == chip)(lambda: arrived(pl.ds(sibling, 1), source_chip))
             for c in range(CHUNKS):
                 a = returned[phase, 2 * source_chip + phase, c].astype(F32)
                 b = returned[phase, 2 * source_chip + 1 - phase, c].astype(F32)
@@ -636,7 +634,7 @@
                 src_ref=others,
                 dst_ref=others,
                 send_sem=out_s.at[phase],
-                recv_sem=out_r.at[phase, chip],
+                recv_sem=out_r.at[chip],
                 device_id={"mem": sibling},
                 device_id_type=MESH,
             ).wait_send()
@@ -687,7 +685,7 @@
             dma((2,)), dma((2, len(PARTS))),
             dma((2,)), dma((2, len(PARTS))),
             dma, dma,
-            dma((2,)), dma((2, 8)),
+            dma((2,)), dma((9,)),
             dma,
         ],
         compiler_params=pltpu.CompilerParams(

time: 69.2 us -> 69 us (level)
  no operation moved by 1% of the time
where the time goes in v7:
time: 69 us; the launch traced here: 68.9 us
  Pallas kernels  68.9 us (100%)
    pallas_call x1, Pallas kernels, per_device(): pl.pallas_call(kernel, out_shape=jax.ShapeDtypeStruct(background.shape, B...  66.8 us
    pallas_call x1, Pallas kernels, per_device(): pl.pallas_call(hand_over, grid=(2,), out_shape=jax.ShapeDtypeStruct(backg...  2.05 us

profile of v7, /device:TPU:1, one launch (start us, length us, event | category | flops | bytes accessed | tf_op | source)
XLA Modules:
  0.0 68.9 jit_solution(8218743309220843053)
XLA Ops:
  0.0 66.8 %analysis.1.in_ref = bf16[16,16,2048]{2,1,0:T(8,128)(2,1)} custom-call(bf16[16,16,2048]{2,1,0:T(8,128)(2,1)} %x_hbm.1, f32[1,2,384]{2,1,0:T(2,128)} %obs_hbm.1, f32[1,2,384]{2,1,0:T(2,128)} %coef_hbm.1, f32[1,2,384]{2,1,0:T(2,128)} %rinv_hbm.1, s32[1,2,384]{2,1,0:T(2,128)} %site_hbm.1, s32[1,2]{1,0:T(1,128)} %count_hbm.1, s32[1,2,5]{2,1,0:T(2,128)} %near_hbm.1), custom_call_target="tpu_custom_call" | custom-call | tf_op jit(solution)/shard_map/analysis/pallas_call | solution.py:651
  66.8 2.1 %hand_over.1 = bf16[16,16,2048]{2,1,0:T(8,128)(2,1)} custom-call(bf16[16,16,2048]{2,1,0:T(8,128)(2,1)} %analysis.1.in_ref), custom_call_target="tpu_custom_call" | custom-call | tf_op jit(solution)/shard_map/hand_over/pallas_call | solution.py:697

commit v8 on v7

--- a/solution.py
+++ b/solution.py
@@ -21,7 +21,7 @@
 PARTS = ((0, 128), (128, MSG))
 CODE_ROW = 5
 SENDS = tuple((away, core) for away in (4, 3, -3, 2, -2, 1, -1) for core in range(2)) + ((0, 0),)
-EARLY = 6
+EARLY = 10
 
 
 def dot(a, b):
@@ -398,13 +398,13 @@
             src_ref=gmsg.at[0, rows] if phase == 0 else xsend.at[side, rows],
             dst_ref=xrecv.at[phase, side, rows],
             send_sem=x_s.at[phase],
-            recv_sem=x_r.at[phase, part],
+            recv_sem=x_r.at[part if phase == 0 else 2],
             device_id={"reg": above if side == 0 else below},
             device_id_type=MESH,
         )
 
     def x_wait(phase, rows, part, sent):
-        sides_wait(xrecv.at[phase, :, rows], x_s.at[phase], x_r.at[phase, part], sent)
+        sides_wait(xrecv.at[phase, :, rows], x_s.at[phase], x_r.at[part if phase == 0 else 2], sent)
 
     def turn_copy(side):
         return pltpu.make_async_remote_copy(
@@ -605,8 +605,7 @@
         keep_own(0)
         center_state(1)
     with stage("x_wait1"):
-        for part in range(len(PARTS)):
-            x_wait(1, slice(*PARTS[part]), part, False)
+        x_wait(1, slice(0, MSG), 0, False)
     with stage("transform1"):
         weights = transform(1)
     with stage("apply1"):
@@ -683,7 +682,7 @@
             dma((2,)), dma((2,)),
             dma((2,)), dma((2,)),
             dma((2,)), dma((2, len(PARTS))),
-            dma((2,)), dma((2, len(PARTS))),
+            dma((2,)), dma((3,)),
             dma, dma,
             dma((2,)), dma((9,)),
             dma,

time: 69 us -> 69 us (level)
  no operation moved by 1% of the time
where the time goes in v8:
time: 69 us; the launch traced here: 68.9 us
  Pallas kernels  68.9 us (100%)
    pallas_call x1, Pallas kernels, per_device(): pl.pallas_call(kernel, out_shape=jax.ShapeDtypeStruct(background.shape, B...  66.8 us
    pallas_call x1, Pallas kernels, per_device(): pl.pallas_call(hand_over, grid=(2,), out_shape=jax.ShapeDtypeStruct(backg...  2.05 us

profile of v8, /device:TPU:1, one launch (start us, length us, event | category | flops | bytes accessed | tf_op | source)
XLA Modules:
  0.0 68.9 jit_solution(10805425934470953352)
XLA Ops:
  0.0 66.8 %analysis.1.in_ref = bf16[16,16,2048]{2,1,0:T(8,128)(2,1)} custom-call(bf16[16,16,2048]{2,1,0:T(8,128)(2,1)} %x_hbm.1, f32[1,2,384]{2,1,0:T(2,128)} %obs_hbm.1, f32[1,2,384]{2,1,0:T(2,128)} %coef_hbm.1, f32[1,2,384]{2,1,0:T(2,128)} %rinv_hbm.1, s32[1,2,384]{2,1,0:T(2,128)} %site_hbm.1, s32[1,2]{1,0:T(1,128)} %count_hbm.1, s32[1,2,5]{2,1,0:T(2,128)} %near_hbm.1), custom_call_target="tpu_custom_call" | custom-call | tf_op jit(solution)/shard_map/analysis/pallas_call | solution.py:650
  66.8 2.1 %hand_over.1 = bf16[16,16,2048]{2,1,0:T(8,128)(2,1)} custom-call(bf16[16,16,2048]{2,1,0:T(8,128)(2,1)} %analysis.1.in_ref), custom_call_target="tpu_custom_call" | custom-call | tf_op jit(solution)/shard_map/hand_over/pallas_call | solution.py:696
